TPU v7x, 32 devices: a whole 2x2x4 slice. The times are simulated.
32 devices in a mesh: gx: 4 (over y, core), gy: 8 (over z, x).
Axes of the slice: x: 2, y: 2, z: 4, core: 2. Of those that a mesh axis runs over, the one named last changes fastest.
Arguments:
- owned_surplus: float32 [4096, 16, 256], P(('gx', 'gy')), may hold values from -0.6 to 0.6
- tile_owner: int32 [4096], replicated, may hold values from 0 to 31, as said below
- grid_levels: int32 [8, 2], replicated, may hold values from 0 to 3, as said below
- coefficients: int32 [8], replicated, may hold values from 1 to 3
- faulty_grids: int32 [2], replicated, may hold values from 1 to 7
- velocity_x: float32 [2048, 8192], P('gx', 'gy'), may hold values from -1 to 1
- velocity_y: float32 [2048, 8192], P('gx', 'gy'), may hold values from -1 to 1
Outputs:
- solution: float32 [2048, 8192], P('gx', 'gy')
Inputs may be any that keep to these rules, and one draw needn't show every extreme that they name: tile_owner[d * 128 + k] = (d + o_k) mod (the number of devices), with offsets o_k that depend only on k; no offset value serves more than 8 of the 128 values of k, and some offset value serves exactly 8. `grid_levels`: row 0 is (0, 0), the full grid.
All inputs are finite; a program needn't handle non-finite values.
Results may differ from a plain program's by a relative error of at most 0.00011.
Values sent between devices are 32-bit elements; how exact they have to be, the bound alone decides.
A program may use at most 128 MiB of HBM per device.

v0:
```python
import jax
import jax.numpy as jnp
from jax import lax
from jax.sharding import PartitionSpec as P

STEPS = 2


TIME_STEP = 0.2
DIFFUSION = 0.5


def padded_2(array, sides, width):
    for axis, dim in sides:
        size, length = (lax.axis_size(axis), array.shape[dim])
        up = [(i, (i + 1) % size) for i in range(size)]
        down = [(j, i) for i, j in up]
        last = lax.slice_in_dim(array, length - width, length, axis=dim)
        initial = lax.slice_in_dim(array, 0, width, axis=dim)
        before = lax.ppermute(last, axis, up)
        after = lax.ppermute(initial, axis, down)
        array = jnp.concatenate([before, array, after], axis=dim)
    return array


def level_of(index_row, top_level):
    result = jnp.full(index_row.shape, top_level, jnp.int32)
    for bit_pos in range(1, top_level + 1):
        result = jnp.where(index_row % 2**bit_pos == 0, top_level - bit_pos, result)
    return result


def weight_table(grid_levels, coefficients, faulty_grids, top_x, top_y):
    grid_count = coefficients.shape[0]
    grid_ids = jnp.arange(grid_count, dtype=jnp.int32)
    alive_mask = jnp.all(faulty_grids[None, :] != grid_ids[:, None], axis=1)
    grid_share = jnp.where(alive_mask, coefficients, 0).astype(jnp.float32)
    covers_x = (
        jnp.arange(top_x + 1, dtype=jnp.int32)[:, None] <= top_x - grid_levels[None, :, 0]
    ).astype(jnp.float32)
    covers_y = (
        jnp.arange(top_y + 1, dtype=jnp.int32)[:, None] <= top_y - grid_levels[None, :, 1]
    ).astype(jnp.float32)
    return jnp.dot(covers_x * grid_share[None, :], covers_y.T, precision=lax.Precision.HIGHEST)


def refine(values, ends_next):
    spacing = values.shape[0] // 2
    while spacing >= 1:
        corners = jnp.concatenate([values[0 :: 2 * spacing], ends_next], axis=0)
        middle = values[spacing :: 2 * spacing]
        values = values.at[spacing :: 2 * spacing].set(middle + 0.5 * (corners[:-1] + corners[1:]))
        spacing = spacing // 2
    return values


def rates(padded, vel_x, vel_y):
    centre = padded[2:-2, 2:-2]
    east_one = padded[3:-1, 2:-2]
    west_one = padded[1:-3, 2:-2]
    east_two = padded[4:, 2:-2]
    west_two = padded[:-4, 2:-2]
    north_one = padded[2:-2, 3:-1]
    south_one = padded[2:-2, 1:-3]
    north_two = padded[2:-2, 4:]
    south_two = padded[2:-2, :-4]
    slope_x = (8.0 * (east_one - west_one) - (east_two - west_two)) / 12.0
    slope_y = (8.0 * (north_one - south_one) - (north_two - south_two)) / 12.0
    curve_x = (16.0 * (east_one + west_one) - (east_two + west_two) - 30.0 * centre) / 12.0
    curve_y = (16.0 * (north_one + south_one) - (north_two + south_two) - 30.0 * centre) / 12.0
    return DIFFUSION * (curve_x + curve_y) - vel_x * slope_x - vel_y * slope_y


def section_rate(field_in, vel_x, vel_y):
    padded = padded_2(field_in, (("gx", 0), ("gy", 1)), 2)
    return rates(padded, vel_x, vel_y)


def one_hot(levels_row, top_level):
    return (levels_row[:, None] == jnp.arange(top_level + 1, dtype=jnp.int32)[None, :]).astype(
        jnp.float32
    )


def local(
    owned_surplus, tile_owner, grid_levels, coefficients, faulty_grids, velocity_x, velocity_y
):
    slot_count, tile_height, tile_width = owned_surplus.shape
    rows_local, cols_local = velocity_x.shape
    size_x = lax.axis_size("gx")
    size_y = lax.axis_size("gy")
    device_count = size_x * size_y
    capacity = 2 * slot_count // device_count
    index_x = lax.axis_index("gx")
    index_y = lax.axis_index("gy")
    own_index = index_x * size_y + index_y
    offsets = tile_owner[:slot_count]
    positions = jnp.arange(slot_count, dtype=jnp.int32)
    same_offset = offsets[:, None] == offsets[None, :]
    earlier = positions[None, :] < positions[:, None]
    slot_rank = jnp.sum((same_offset & earlier).astype(jnp.int32), axis=1)
    target = (own_index - offsets) % device_count
    outgoing = jnp.zeros((device_count * capacity, tile_height, tile_width), jnp.float32)
    outgoing = outgoing.at[target * capacity + slot_rank].set(owned_surplus)
    incoming = lax.all_to_all(
        outgoing.reshape(device_count, capacity, tile_height, tile_width),
        ("gx", "gy"),
        split_axis=0,
        concat_axis=0,
        tiled=True,
    )
    incoming = incoming.reshape(device_count * capacity, tile_height, tile_width)
    source = (own_index + offsets) % device_count
    tile_data = jnp.take(incoming, source * capacity + slot_rank, axis=0)
    block = tile_data.reshape(
        rows_local // tile_height, cols_local // tile_width, tile_height, tile_width
    )
    block = block.transpose(0, 2, 1, 3).reshape(rows_local, cols_local)
    top_x = (rows_local * size_x).bit_length() - 1
    top_y = (cols_local * size_y).bit_length() - 1
    table = weight_table(grid_levels, coefficients, faulty_grids, top_x, top_y)
    global_rows = index_x * rows_local + jnp.arange(rows_local, dtype=jnp.int32)
    global_cols = index_y * cols_local + jnp.arange(cols_local, dtype=jnp.int32)
    hot_rows = one_hot(level_of(global_rows, top_x), top_x)
    hot_cols = one_hot(level_of(global_cols, top_y), top_y)
    row_weights = jnp.dot(hot_rows, table, precision=lax.Precision.HIGHEST)
    weights = jnp.dot(row_weights, hot_cols.T, precision=lax.Precision.HIGHEST)
    surplus = block * weights
    skeleton_x = lax.all_gather(surplus[0:1], "gx", axis=0, tiled=True)
    coarse_x = refine(skeleton_x, skeleton_x[0:1])
    own_row = lax.dynamic_slice_in_dim(coarse_x, index_x, 1, 0)
    next_row = lax.dynamic_slice_in_dim(coarse_x, (index_x + 1) % size_x, 1, 0)
    nodal_x = refine(surplus.at[0:1].set(own_row), next_row)
    skeleton_y = lax.all_gather(nodal_x[:, 0:1], "gy", axis=1, tiled=True).T
    coarse_y = refine(skeleton_y, skeleton_y[0:1])
    own_col = lax.dynamic_slice_in_dim(coarse_y, index_y, 1, 0)
    next_col = lax.dynamic_slice_in_dim(coarse_y, (index_y + 1) % size_y, 1, 0)
    flipped = nodal_x.T
    nodal = refine(flipped.at[0:1].set(own_col), next_col).T
    field_now = nodal
    for step_index in range(STEPS):
        first_rate = section_rate(field_now, velocity_x, velocity_y)
        middle_field = field_now + TIME_STEP * first_rate
        second_rate = section_rate(middle_field, velocity_x, velocity_y)
        field_now = 0.5 * (field_now + middle_field + TIME_STEP * second_rate)
    return field_now


def solution(mesh):
    return jax.shard_map(
        local,
        mesh=mesh,
        in_specs=(P(("gx", "gy"), None, None), P(), P(), P(), P(), P("gx", "gy"), P("gx", "gy")),
        out_specs=P("gx", "gy"),
        check_vma=False,
    )
```

profile of v0, /device:TPU:0, one launch (start us, length us, event | category | flops | bytes accessed | tf_op | source)
XLA Modules:
  0.0 329.6 jit_solution(13549357123453492636)
XLA Ops:
  1.6 2.5 broadcast_in_dim.134
  4.1 15.7 %scatter_fusion = f32[256,16,256]{2,1,0:T(8,128)} fusion(f32[256,16,256]{2,1,0:T(8,128)} %broadcast_in_dim.134, s32[128]{0:T(128)S(1)} %get-tuple-element.109, f32[128,16,256]{2,1,0:T(8,128)S(1)} %copy-done.3), kind=kCustom, calls=%fused_computation.1 | custom fusion | bytes 6291968 | tf_op jit(solution)/shard_map/scatter | solution.py:104
  19.8 7.4 %all-to-all-start = ((f32[32,8,16,256]{3,2,1,0:T(8,128)}), f32[32,8,16,256]{3,2,1,0:T(8,128)}, u32[]{:S(2)}, u32[]{:S(2)}) async-start(f32[32,8,16,256]{3,2,1,0:T(8,128)} %bitcast.106), calls=%async_computation | async-start | bytes 8388608 | tf_op jit(solution)/shard_map/all_to_all | solution.py:105
  28.4 94.0 %all-to-all-done = f32[32,8,16,256]{3,2,1,0:T(8,128)} async-done(((f32[32,8,16,256]{3,2,1,0:T(8,128)}), f32[32,8,16,256]{3,2,1,0:T(8,128)}, u32[]{:S(2)}, u32[]{:S(2)}) %all-to-all-start) | async-done | bytes 4194336 | tf_op jit(solution)/shard_map/all_to_all | solution.py:105
  122.4 2.9 gather_fusion
  129.1 5.2 %all-gather = f32[4,1,1024]{2,1,0:T(1,128)S(1)} all-gather(f32[1,1,1024]{2,1,0:T(1,128)S(1)} %slice_bitcast_fusion.2), channel_id=1, replica_groups=mesh['gx'=4,'gy'=8] {'gx'}, dimensions={0}, use_global_device_ids=true | all-gather | bytes 20480 | tf_op jit(solution)/shard_map/all_gather | solution.py:129
  146.2 1.9 scatter_custom_fusion.8
  148.7 2.8 slice.532
  151.5 3.2 scatter_custom_fusion.9
  156.2 1.9 copy.178
  158.1 26.0 %all-gather.1 = f32[8,1,512]{2,1,0:T(1,128)S(1)} all-gather(f32[1,1,512]{2,1,0:T(1,128)S(1)} %bitcast.112), channel_id=1, replica_groups=mesh['gx'=4,'gy'=8] {'gy'}, dimensions={0}, use_global_device_ids=true | all-gather | bytes 18432 | tf_op jit(solution)/shard_map/all_gather | solution.py:134
  196.7 1.8 scatter_custom_fusion.18
  200.1 2.3 scatter_custom_fusion.19
  203.4 3.5 %slice.569 = f32[512,512]{1,0:T(8,128)} slice(f32[1024,512]{1,0:T(8,128)S(1)} %scatter_custom_fusion.19), slice={[1:1024:2], [0:512:1]} | slice | bytes 2097152 | tf_op jit(solution)/shard_map/slice | solution.py:51
  206.9 3.9 %scatter_custom_fusion.20 = f32[1024,512]{1,0:T(8,128)S(1)} fusion(f32[1024,512]{1,0:T(8,128)S(1)} %scatter_custom_fusion.19, s32[512]{0:T(512)S(1)} %bitcast.113, f32[512,512]{1,0:T(8,128)} %slice.569, f32[512,512]{1,0:T(8,128)S(1)} %slice.570, f32[1,512]{1,0:T(1,128)S(1)} %get-tuple-element.80, f32[]{:T(128)} %constant.523, f32[]{:T(128)} %constant.514.clone.1), kind=kCustom, calls=%fused_computation.85 | custom fusion | flops 1048576 | bytes 4196360 | tf_op jit(solution)/shard_map/scatter | solution.py:52
  212.8 11.7 %collective-permute-done.1 = f32[2,1024]{0,1:T(8,128)S(1)} collective-permute-done((f32[2,1024]{0,1:T(8,128)S(1)}, f32[2,1024]{0,1:T(8,128)S(1)}, u32[]{:S(2)}, u32[]{:S(2)}) %collective-permute-start.1) | collective-permute-done | bytes 8224 | tf_op jit(solution)/shard_map/ppermute | solution.py:20
  224.6 2.0 collective-permute-start.3
  226.6 2.9 copy.179
  229.5 2.9 copy.180
  234.6 5.8 %fusion.20 = f32[512,1024]{0,1:T(8,128)S(1)} fusion(f32[512,1024]{0,1:T(8,128)S(1)} %bitcast.105, f32[512,1024]{0,1:T(8,128)S(1)} %copy-done.1, f32[512,1024]{0,1:T(8,128)S(1)} %copy-done, f32[516,1026]{0,1:T(8,128)S(1)} %get-tuple-element.98, f32[516,1026]{0,1:T(8,128)S(1)} %get-tuple-element.97, f32[2,1024]{0,1:T(8,128)S(1)} %collective-permute-done, ...), kind=kLoop, calls=%fused_computation.78 | loop fusion | flops 17301504 | bytes 16793600 | tf_op jit(solution)/shard_map/add | solution.py:143
  242.5 11.9 %collective-permute-done.5 = f32[2,1024]{0,1:T(8,128)S(1)} collective-permute-done((f32[2,1024]{0,1:T(8,128)S(1)}, f32[2,1024]{0,1:T(8,128)S(1)}, u32[]{:S(2)}, u32[]{:S(2)}) %collective-permute-start.5) | collective-permute-done | bytes 8224 | tf_op jit(solution)/shard_map/ppermute | solution.py:20
  254.4 2.8 collective-permute-start.6
  258.6 5.0 %collective-permute-done.7 = f32[516,2]{0,1:T(2,128)S(1)} collective-permute-done((f32[516,2]{0,1:T(2,128)S(1)}, f32[516,2]{0,1:T(2,128)S(1)}, u32[]{:S(2)}, u32[]{:S(2)}) %collective-permute-start.7) | collective-permute-done | bytes 4160 | tf_op jit(solution)/shard_map/ppermute | solution.py:20
  265.3 5.9 %broadcast_multiply_fusion = (f32[512,1024]{0,1:T(8,128)S(1)}, f32[512,1024]{0,1:T(8,128)S(1)}) fusion(f32[512,1024]{0,1:T(8,128)S(1)} %copy-done.1, f32[512,1024]{0,1:T(8,128)S(1)} %copy-done, f32[516,1026]{0,1:T(8,128)S(1)} %get-tuple-element.94, f32[516,1026]{0,1:T(8,128)S(1)} %get-tuple-element.93, f32[512,1024]{0,1:T(8,128)S(1)} %fusion.20, ...), kind=kLoop, calls=%fused_computation.93 | loop fusion | flops 18350080 | bytes 20987904 | tf_op jit(solution)/shard_map/mul | solution.py:145
  273.1 12.1 %collective-permute-done.9 = f32[2,1024]{0,1:T(8,128)S(1)} collective-permute-done((f32[2,1024]{0,1:T(8,128)S(1)}, f32[2,1024]{0,1:T(8,128)S(1)}, u32[]{:S(2)}, u32[]{:S(2)}) %collective-permute-start.9) | collective-permute-done | bytes 8224 | tf_op jit(solution)/shard_map/ppermute | solution.py:20
  285.4 2.0 collective-permute-start.11
  289.0 2.8 collective-permute-done.11
  293.5 5.8 %fusion.14 = f32[512,1024]{0,1:T(8,128)S(1)} fusion(f32[512,1024]{0,1:T(8,128)S(1)} %get-tuple-element.77, f32[512,1024]{0,1:T(8,128)S(1)} %copy-done.1, f32[512,1024]{0,1:T(8,128)S(1)} %copy-done, f32[516,1026]{0,1:T(8,128)S(1)} %get-tuple-element.90, f32[516,1026]{0,1:T(8,128)S(1)} %get-tuple-element.89, f32[512,1024]{0,1:T(8,128)S(1)} %get-tuple-element.78, ...), kind=kLoop, calls=%fused_computation.70 | loop fusion | flops 17301504 | bytes 18890752 | tf_op jit(solution)/shard_map/add | solution.py:143
  301.2 12.3 %collective-permute-done.13 = f32[2,1024]{0,1:T(8,128)S(1)} collective-permute-done((f32[2,1024]{0,1:T(8,128)S(1)}, f32[2,1024]{0,1:T(8,128)S(1)}, u32[]{:S(2)}, u32[]{:S(2)}) %collective-permute-start.13) | collective-permute-done | bytes 8224 | tf_op jit(solution)/shard_map/ppermute | solution.py:20
  313.7 2.0 collective-permute-start.15
  317.3 3.0 collective-permute-done.15
  322.0 5.8 %fusion.11 = f32[512,1024]{0,1:T(8,128)S(1)} fusion(f32[512,1024]{0,1:T(8,128)S(1)} %copy-done.1, f32[512,1024]{0,1:T(8,128)S(1)} %copy-done, f32[516,1026]{0,1:T(8,128)S(1)} %get-tuple-element.86, f32[516,1026]{0,1:T(8,128)S(1)} %get-tuple-element.85, f32[512,1024]{0,1:T(8,128)S(1)} %fusion.14, f32[2,1024]{0,1:T(8,128)S(1)} %collective-permute-done.12, ...), kind=kLoop, calls=%fused_computation.66 | loop fusion | flops 18874368 | bytes 18890752 | tf_op jit(solution)/shard_map/mul | solution.py:145
  (157 shorter events, 57.0 us)
Async XLA Ops:
  1.6 2.5 copy-start.3
  19.8 8.0 %copy-start.5 = (s32[2]{0:T(128)S(1)}, s32[2]{0:T(128)}, u32[]{:S(2)}) copy-start(s32[2]{0:T(128)} %param.23) | copy-start | bytes 28
  19.8 8.1 %copy-start.6 = (s32[8]{0:T(128)S(1)}, s32[8]{0:T(128)}, u32[]{:S(2)}) copy-start(s32[8]{0:T(128)} %param.22) | copy-start | bytes 100
  19.8 8.1 %copy-start.4 = (s32[8,2]{0,1:T(2,128)S(1)}, s32[8,2]{0,1:T(2,128)}, u32[]{:S(2)}) copy-start(s32[8,2]{0,1:T(2,128)} %param.21) | copy-start | bytes 196
  19.8 102.6 %all-to-all-start = ((f32[32,8,16,256]{3,2,1,0:T(8,128)}), f32[32,8,16,256]{3,2,1,0:T(8,128)}, u32[]{:S(2)}, u32[]{:S(2)}) async-start(f32[32,8,16,256]{3,2,1,0:T(8,128)} %bitcast.106), calls=%async_computation | async-start | bytes 8388608 | tf_op jit(solution)/shard_map/all_to_all | solution.py:105
  154.7 1.3 copy-start.2
  211.0 13.5 %collective-permute-start.1 = (f32[2,1024]{0,1:T(8,128)S(1)}, f32[2,1024]{0,1:T(8,128)S(1)}, u32[]{:S(2)}, u32[]{:S(2)}) collective-permute-start(f32[2,1024]{0,1:T(8,128)S(1)} %get-tuple-element.107), channel_id=1, source_target_pairs={{0,8},{8,16},{16,24},{24,0},{1,9},{9,17},{17,25},{25,1},{2,10},{10... | collective-permute-start | bytes 24584 | tf_op jit(solution)/shard_map/ppermute | solution.py:20
  211.1 13.4 %collective-permute-start = (f32[2,1024]{0,1:T(8,128)S(1)}, f32[2,1024]{0,1:T(8,128)S(1)}, u32[]{:S(2)}, u32[]{:S(2)}) collective-permute-start(f32[2,1024]{0,1:T(8,128)S(1)} %get-tuple-element.108), channel_id=1, source_target_pairs={{8,0},{16,8},{24,16},{0,24},{9,1},{17,9},{25,17},{1,25},{10,2},{18... | collective-permute-start | bytes 24584 | tf_op jit(solution)/shard_map/ppermute | solution.py:21
  224.5 7.9 %collective-permute-start.2 = (f32[516,2]{0,1:T(2,128)S(1)}, f32[516,2]{0,1:T(2,128)S(1)}, u32[]{:S(2)}, u32[]{:S(2)}) collective-permute-start(f32[516,2]{0,1:T(2,128)S(1)} %get-tuple-element.99), channel_id=1, source_target_pairs={{1,0},{2,1},{3,2},{4,3},{5,4},{6,5},{7,6},{0,7},{9,8},{10,9},{11,1... | collective-permute-start | bytes 12392 | tf_op jit(solution)/shard_map/ppermute | solution.py:21
  224.6 7.8 %collective-permute-start.3 = (f32[516,2]{0,1:T(2,128)S(1)}, f32[516,2]{0,1:T(2,128)S(1)}, u32[]{:S(2)}, u32[]{:S(2)}) collective-permute-start(f32[516,2]{0,1:T(2,128)S(1)} %get-tuple-element.100), channel_id=1, source_target_pairs={{0,1},{1,2},{2,3},{3,4},{4,5},{5,6},{6,7},{7,0},{8,9},{9,10},{10,1... | collective-permute-start | bytes 12392 | tf_op jit(solution)/shard_map/ppermute | solution.py:20
  232.4 1.7 copy-start
  232.4 2.2 copy-start.1
  240.7 13.7 %collective-permute-start.5 = (f32[2,1024]{0,1:T(8,128)S(1)}, f32[2,1024]{0,1:T(8,128)S(1)}, u32[]{:S(2)}, u32[]{:S(2)}) collective-permute-start(f32[2,1024]{0,1:T(8,128)S(1)} %get-tuple-element.105), channel_id=1, source_target_pairs={{0,8},{8,16},{16,24},{24,0},{1,9},{9,17},{17,25},{25,1},{2,10},{10... | collective-permute-start | bytes 24584 | tf_op jit(solution)/shard_map/ppermute | solution.py:20
  240.8 13.6 %collective-permute-start.4 = (f32[2,1024]{0,1:T(8,128)S(1)}, f32[2,1024]{0,1:T(8,128)S(1)}, u32[]{:S(2)}, u32[]{:S(2)}) collective-permute-start(f32[2,1024]{0,1:T(8,128)S(1)} %get-tuple-element.106), channel_id=1, source_target_pairs={{8,0},{16,8},{24,16},{0,24},{9,1},{17,9},{25,17},{1,25},{10,2},{18... | collective-permute-start | bytes 24584 | tf_op jit(solution)/shard_map/ppermute | solution.py:21
  254.4 4.1 %collective-permute-start.6 = (f32[516,2]{0,1:T(2,128)S(1)}, f32[516,2]{0,1:T(2,128)S(1)}, u32[]{:S(2)}, u32[]{:S(2)}) collective-permute-start(f32[516,2]{0,1:T(2,128)S(1)} %get-tuple-element.95), channel_id=1, source_target_pairs={{1,0},{2,1},{3,2},{4,3},{5,4},{6,5},{7,6},{0,7},{9,8},{10,9},{11,1... | collective-permute-start | bytes 12392 | tf_op jit(solution)/shard_map/ppermute | solution.py:21
  257.2 6.3 %collective-permute-start.7 = (f32[516,2]{0,1:T(2,128)S(1)}, f32[516,2]{0,1:T(2,128)S(1)}, u32[]{:S(2)}, u32[]{:S(2)}) collective-permute-start(f32[516,2]{0,1:T(2,128)S(1)} %get-tuple-element.96), channel_id=1, source_target_pairs={{0,1},{1,2},{2,3},{3,4},{4,5},{5,6},{6,7},{7,0},{8,9},{9,10},{10,1... | collective-permute-start | bytes 12392 | tf_op jit(solution)/shard_map/ppermute | solution.py:20
  271.3 13.9 %collective-permute-start.9 = (f32[2,1024]{0,1:T(8,128)S(1)}, f32[2,1024]{0,1:T(8,128)S(1)}, u32[]{:S(2)}, u32[]{:S(2)}) collective-permute-start(f32[2,1024]{0,1:T(8,128)S(1)} %get-tuple-element.103), channel_id=1, source_target_pairs={{0,8},{8,16},{16,24},{24,0},{1,9},{9,17},{17,25},{25,1},{2,10},{10... | collective-permute-start | bytes 24584 | tf_op jit(solution)/shard_map/ppermute | solution.py:20
  271.4 13.9 %collective-permute-start.8 = (f32[2,1024]{0,1:T(8,128)S(1)}, f32[2,1024]{0,1:T(8,128)S(1)}, u32[]{:S(2)}, u32[]{:S(2)}) collective-permute-start(f32[2,1024]{0,1:T(8,128)S(1)} %get-tuple-element.104), channel_id=1, source_target_pairs={{8,0},{16,8},{24,16},{0,24},{9,1},{17,9},{25,17},{1,25},{10,2},{18... | collective-permute-start | bytes 24584 | tf_op jit(solution)/shard_map/ppermute | solution.py:21
  285.3 3.6 %collective-permute-start.10 = (f32[516,2]{0,1:T(2,128)S(1)}, f32[516,2]{0,1:T(2,128)S(1)}, u32[]{:S(2)}, u32[]{:S(2)}) collective-permute-start(f32[516,2]{0,1:T(2,128)S(1)} %get-tuple-element.91), channel_id=1, source_target_pairs={{1,0},{2,1},{3,2},{4,3},{5,4},{6,5},{7,6},{0,7},{9,8},{10,9},{11,1... | collective-permute-start | bytes 12392 | tf_op jit(solution)/shard_map/ppermute | solution.py:21
  285.4 6.4 %collective-permute-start.11 = (f32[516,2]{0,1:T(2,128)S(1)}, f32[516,2]{0,1:T(2,128)S(1)}, u32[]{:S(2)}, u32[]{:S(2)}) collective-permute-start(f32[516,2]{0,1:T(2,128)S(1)} %get-tuple-element.92), channel_id=1, source_target_pairs={{0,1},{1,2},{2,3},{3,4},{4,5},{5,6},{6,7},{7,0},{8,9},{9,10},{10,1... | collective-permute-start | bytes 12392 | tf_op jit(solution)/shard_map/ppermute | solution.py:20
  299.4 14.1 %collective-permute-start.13 = (f32[2,1024]{0,1:T(8,128)S(1)}, f32[2,1024]{0,1:T(8,128)S(1)}, u32[]{:S(2)}, u32[]{:S(2)}) collective-permute-start(f32[2,1024]{0,1:T(8,128)S(1)} %get-tuple-element.101), channel_id=1, source_target_pairs={{0,8},{8,16},{16,24},{24,0},{1,9},{9,17},{17,25},{25,1},{2,10},{10... | collective-permute-start | bytes 24584 | tf_op jit(solution)/shard_map/ppermute | solution.py:20
  299.5 14.0 %collective-permute-start.12 = (f32[2,1024]{0,1:T(8,128)S(1)}, f32[2,1024]{0,1:T(8,128)S(1)}, u32[]{:S(2)}, u32[]{:S(2)}) collective-permute-start(f32[2,1024]{0,1:T(8,128)S(1)} %get-tuple-element.102), channel_id=1, source_target_pairs={{8,0},{16,8},{24,16},{0,24},{9,1},{17,9},{25,17},{1,25},{10,2},{18... | collective-permute-start | bytes 24584 | tf_op jit(solution)/shard_map/ppermute | solution.py:21
  313.6 3.6 %collective-permute-start.14 = (f32[516,2]{0,1:T(2,128)S(1)}, f32[516,2]{0,1:T(2,128)S(1)}, u32[]{:S(2)}, u32[]{:S(2)}) collective-permute-start(f32[516,2]{0,1:T(2,128)S(1)} %get-tuple-element.87), channel_id=1, source_target_pairs={{1,0},{2,1},{3,2},{4,3},{5,4},{6,5},{7,6},{0,7},{9,8},{10,9},{11,1... | collective-permute-start | bytes 12392 | tf_op jit(solution)/shard_map/ppermute | solution.py:21
  313.7 6.6 %collective-permute-start.15 = (f32[516,2]{0,1:T(2,128)S(1)}, f32[516,2]{0,1:T(2,128)S(1)}, u32[]{:S(2)}, u32[]{:S(2)}) collective-permute-start(f32[516,2]{0,1:T(2,128)S(1)} %get-tuple-element.88), channel_id=1, source_target_pairs={{0,1},{1,2},{2,3},{3,4},{4,5},{5,6},{6,7},{7,0},{8,9},{9,10},{10,1... | collective-permute-start | bytes 12392 | tf_op jit(solution)/shard_map/ppermute | solution.py:20
where the time goes:
time: 331 us; the launch traced here: 330 us
  waiting for transfers between devices  157 us (47%)
  other arithmetic  64.8 us (20%)
  local copies, waits for them, and re-layouts  50.3 us (15%)
  blocking collectives  31.2 us (9%)
  starting transfers between devices  23.5 us (7%)
    all_to_all x1, waiting for transfers between devices, local(): lax.all_to_all(outgoing.reshape(device_count, capacity, tile_height, tile...  94 us
    ppermute x8, waiting for transfers between devices, padded_2(): before = lax.ppermute(last, axis, up)  58.7 us
    scatter x20, other arithmetic, refine(): values.at[spacing::2 * spacing]  32.9 us
    all_gather x1, blocking collectives, local(): skeleton_y = lax.all_gather(nodal_x[:, 0:1], 'gy', axis=1, tiled=True).T  26 us
    scatter x1, local copies, waits for them, and re-layouts, local(): outgoing = outgoing.at[target * capacity + slot_rank].set(owned_surplus)  15.7 us
    mul x2, other arithmetic, local(): field_now = 0.5 * (field_now + middle_field + TIME_STEP * second_rate)  11.6 us
    add x2, other arithmetic, local(): middle_field = field_now + TIME_STEP * first_rate  11.6 us
    ppermute x8, starting transfers between devices, padded_2(): after = lax.ppermute(initial, axis, down)  9.76 us
  transfers between devices with their start and end apart: 17, of which 11 were waited for; matrix products, arithmetic and copies ran while one was open for 2% of the time, Pallas kernels for 0%

commit v1 on v0

v1 whole, which is shorter than its diff:
```python
import functools

import jax
import jax.numpy as jnp
import ml_dtypes
import numpy as np
from jax import lax
from jax.experimental import pallas as pl
from jax.experimental.pallas import tpu as pltpu
from jax.sharding import PartitionSpec as P

STEPS = 2
TIME_STEP = 0.2
CHUNK = 256
HALO = 8
TOP = 16
MESH = pl.DeviceIdType.MESH


def hat_matrix():
    points = np.arange(CHUNK)[:, None]
    nodes = np.arange(CHUNK)[None, :]
    reach = np.where(nodes == 0, 1, nodes & -nodes)
    hats = np.maximum(0.0, 1.0 - np.abs(points - nodes) / reach)
    hats[:, 0] = 0.0
    return hats


def coarse_matrix(count):
    values = np.eye(count)
    spacing = count // 2
    while spacing >= 1:
        for x in range(spacing, count, 2 * spacing):
            values[x] += 0.5 * (values[x - spacing] + values[(x + spacing) % count])
        spacing //= 2
    return values


def coarse_rows(size, per_device):
    full = coarse_matrix(size * per_device)
    table = np.zeros((size, 8, size * 8))
    for me in range(size):
        for row in range(per_device + 1):
            point = (me * per_device + row) % (size * per_device)
            for j in range(size * per_device):
                table[me, row, (j // per_device) * 8 + j % per_device] = full[point, j]
    return table.astype(np.float32)


def split_dot(matrix, values, left):
    high = values.astype(jnp.bfloat16)
    low = (values - high.astype(jnp.float32)).astype(jnp.bfloat16)
    if left:
        return jnp.dot(matrix, high, preferred_element_type=jnp.float32) + jnp.dot(
            matrix, low, preferred_element_type=jnp.float32
        )
    return jnp.dot(high, matrix, preferred_element_type=jnp.float32) + jnp.dot(
        low, matrix, preferred_element_type=jnp.float32
    )


def exact_dot(a, b):
    return jnp.dot(a, b, precision=lax.Precision.HIGHEST, preferred_element_type=jnp.float32)


def kernel(
    size_x,
    size_y,
    place_ref,
    weight_ref,
    incoming_ref,
    vel_x_ref,
    vel_y_ref,
    hats_ref,
    hats_t_ref,
    coarse_x_ref,
    coarse_y_ref,
    out_ref,
    block,
    fields,
    middle,
    rows_all,
    cols_all,
    col_send,
    col_recv,
    local_sem,
    rows_send_sem,
    rows_recv_sem,
    cols_send_sem,
    cols_recv_sem,
    face_send_sem,
    face_recv_sem,
    side_send_sem,
    side_recv_sem,
):
    rows, cols = out_ref.shape
    tile_rows, tile_cols = weight_ref.shape
    across = cols // tile_cols
    ix = lax.axis_index("gx")
    iy = lax.axis_index("gy")

    loads = [
        pltpu.make_async_copy(
            source, fields.at[f, pl.ds(TOP, rows), pl.ds(0, cols)], local_sem.at[f]
        )
        for f, source in ((1, vel_x_ref), (2, vel_y_ref))
    ]
    for load in loads:
        load.start()

    barrier = pltpu.get_barrier_semaphore()
    for step in range(1, size_x):
        pl.semaphore_signal(
            barrier, inc=1, device_id=(lax.rem(ix + step, size_x), iy), device_id_type=MESH
        )
    for step in range(1, size_y):
        pl.semaphore_signal(
            barrier, inc=1, device_id=(ix, lax.rem(iy + step, size_y)), device_id_type=MESH
        )
    pl.semaphore_wait(barrier, size_x + size_y - 2)

    before_x = (lax.rem(ix + size_x - 1, size_x), iy)
    after_x = (lax.rem(ix + 1, size_x), iy)
    before_y = (ix, lax.rem(iy + size_y - 1, size_y))
    after_y = (ix, lax.rem(iy + 1, size_y))

    def faces(f):
        return [
            pltpu.make_async_remote_copy(
                src_ref=fields.at[f, pl.ds(start, HALO), pl.ds(0, cols)],
                dst_ref=fields.at[f, pl.ds(target, HALO), pl.ds(0, cols)],
                send_sem=face_send_sem.at[f, side],
                recv_sem=face_recv_sem.at[f, side],
                device_id=device,
                device_id_type=MESH,
            )
            for side, start, target, device in (
                (0, TOP, TOP + rows, before_x),
                (1, TOP + rows - HALO, TOP - HALO, after_x),
            )
        ]

    def sides(f):
        col_send[f, 0] = fields[f, :, 0:128].T[0:HALO]
        col_send[f, 1] = fields[f, :, cols - 128 : cols].T[128 - HALO : 128]
        return [
            pltpu.make_async_remote_copy(
                src_ref=col_send.at[f, side],
                dst_ref=col_recv.at[f, side],
                send_sem=side_send_sem.at[f, side],
                recv_sem=side_recv_sem.at[f, side],
                device_id=device,
                device_id_type=MESH,
            )
            for side, device in ((0, before_y), (1, after_y))
        ]

    def fill_sides(f):
        length = col_recv.shape[3]
        strip = jnp.concatenate(
            [
                col_recv[f, 0],
                jnp.zeros((128 - 2 * HALO, length), jnp.float32),
                col_recv[f, 1],
            ],
            axis=0,
        )
        fields[f, :, cols : cols + 128] = strip.T

    for load in loads:
        load.wait()
    vel_faces = faces(1) + faces(2)
    for copy in vel_faces:
        copy.start()

    weight = weight_ref[...]

    def put(kx, carry):
        for ky in range(across):
            start = pl.multiple_of(kx * tile_rows, tile_rows)
            block[pl.ds(start, tile_rows), ky * tile_cols : (ky + 1) * tile_cols] = (
                incoming_ref[place_ref[kx * across + ky]] * weight
            )
        return carry

    lax.fori_loop(0, rows // tile_rows, put, 0)

    chunks_x = rows // CHUNK
    chunks_y = cols // CHUNK
    rows_all[ix] = jnp.concatenate(
        [block[c * CHUNK : c * CHUNK + 1, :] for c in range(chunks_x)]
        + [jnp.zeros((8 - chunks_x, cols), jnp.float32)],
        axis=0,
    )
    row_copies = [
        pltpu.make_async_remote_copy(
            src_ref=rows_all.at[ix],
            dst_ref=rows_all.at[ix],
            send_sem=rows_send_sem.at[step],
            recv_sem=rows_recv_sem.at[step],
            device_id=(lax.rem(ix + step, size_x), iy),
            device_id_type=MESH,
        )
        for step in range(1, size_x)
    ]
    for copy in row_copies:
        copy.start()

    for copy in vel_faces:
        copy.wait()
    vel_sides = sides(1) + sides(2)
    for copy in vel_sides:
        copy.start()

    for copy in row_copies:
        copy.wait()
    corners = exact_dot(coarse_x_ref[ix], rows_all[...].reshape(size_x * 8, cols))
    part = lax.broadcasted_iota(jnp.int32, (CHUNK, 1), 0).astype(jnp.float32) * (1.0 / CHUNK)
    for c in range(chunks_x):
        inner = split_dot(hats_ref[...], block[c * CHUNK : (c + 1) * CHUNK, :], True)
        block[c * CHUNK : (c + 1) * CHUNK, :] = (
            inner + (1.0 - part) * corners[c : c + 1] + part * corners[c + 1 : c + 2]
        )

    lane = lax.broadcasted_iota(jnp.int32, (rows, 128), 1)
    picked = jnp.zeros((rows, 128), jnp.float32)
    for c in range(chunks_y):
        column = block[:, c * CHUNK : c * CHUNK + 1]
        picked = jnp.where(lane == c, column, picked)
    cols_all[iy] = picked.T[0:8]
    col_copies = [
        pltpu.make_async_remote_copy(
            src_ref=cols_all.at[iy],
            dst_ref=cols_all.at[iy],
            send_sem=cols_send_sem.at[step],
            recv_sem=cols_recv_sem.at[step],
            device_id=(ix, lax.rem(iy + step, size_y)),
            device_id_type=MESH,
        )
        for step in range(1, size_y)
    ]
    for copy in col_copies:
        copy.start()

    for c in range(chunks_y):
        span = slice(c * CHUNK, (c + 1) * CHUNK)
        block[:, span] = split_dot(hats_t_ref[...], block[:, span], False)

    for copy in vel_sides:
        copy.wait()
    fill_sides(1)
    fill_sides(2)

    for copy in col_copies:
        copy.wait()
    corners = exact_dot(coarse_y_ref[iy], cols_all[...].reshape(size_y * 8, rows))
    corners = jnp.concatenate([corners, jnp.zeros((120, rows), jnp.float32)], axis=0).T
    part = lax.broadcasted_iota(jnp.int32, (1, CHUNK), 1).astype(jnp.float32) * (1.0 / CHUNK)
    for c in range(chunks_y):
        span = slice(c * CHUNK, (c + 1) * CHUNK)
        fields[0, TOP : TOP + rows, span] = (
            block[:, span]
            + (1.0 - part) * corners[:, c : c + 1]
            + part * corners[:, c + 1 : c + 2]
        )

    own_faces = faces(0)
    for copy in own_faces:
        copy.start()
    for copy in own_faces:
        copy.wait()
    own_sides = sides(0)
    for copy in own_sides:
        copy.start()
    for copy in own_sides:
        copy.wait()
    fill_sides(0)

    width = cols + 128
    scale = TIME_STEP / 12.0

    def change(read, start):
        centre = read(start, 0)
        west_one, east_one = read(start, -1), read(start, 1)
        west_two, east_two = read(start, -2), read(start, 2)
        north_one = pltpu.roll(centre, width - 1, 1)
        south_one = pltpu.roll(centre, 1, 1)
        north_two = pltpu.roll(centre, width - 2, 1)
        south_two = pltpu.roll(centre, 2, 1)
        near = (east_one + west_one) + (north_one + south_one)
        far = (east_two + west_two) + (north_two + south_two)
        slope_x = 8.0 * (east_one - west_one) - (east_two - west_two)
        slope_y = 8.0 * (north_one - south_one) - (north_two - south_two)
        vel_x = fields[1, pl.ds(start, 8), :]
        vel_y = fields[2, pl.ds(start, 8), :]
        total = (8.0 * near - 0.5 * far - 30.0 * centre) - vel_x * slope_x - vel_y * slope_y
        return centre, scale * total

    def read_field(start, shift):
        around = fields.at[0, pl.ds(pl.multiple_of(start - 8, 8), 24), :]
        return around[8 + shift : 16 + shift, :]

    def read_middle(start, shift):
        around = middle.at[pl.ds(pl.multiple_of(start - 8, 8), 24), :]
        return around[8 + shift : 16 + shift, :]

    for step in range(STEPS):
        last = step == STEPS - 1

        def first_half(i, carry):
            start = pl.multiple_of(i * 8, 8)
            centre, delta = change(read_field, start)
            middle[pl.ds(start, 8), :] = centre + delta
            return carry

        lax.fori_loop(TOP // 8 - 1, (TOP + rows) // 8 + 1, first_half, 0)

        def second_half(i, carry):
            start = pl.multiple_of(i * 8, 8)
            centre, delta = change(read_middle, start)
            value = 0.5 * (fields[0, pl.ds(start, 8), :] + centre + delta)
            if last:
                out_ref[pl.ds(pl.multiple_of(start - TOP, 8), 8), :] = value[:, :cols]
            else:
                fields[0, pl.ds(start, 8), :] = value
            return carry

        edge = 0 if last else 1
        lax.fori_loop(TOP // 8 - edge, (TOP + rows) // 8 + edge, second_half, 0)


def restart(place, weight, incoming, vel_x, vel_y, size_x, size_y):
    rows, cols = vel_x.shape
    frame = (rows + 2 * TOP + 127) // 128 * 128
    hats = hat_matrix()
    operands = (
        place,
        weight,
        incoming,
        vel_x,
        vel_y,
        jnp.asarray(hats.astype(ml_dtypes.bfloat16)),
        jnp.asarray(hats.T.astype(ml_dtypes.bfloat16)),
        jnp.asarray(coarse_rows(size_x, rows // CHUNK)),
        jnp.asarray(coarse_rows(size_y, cols // CHUNK)),
    )
    vmem = pl.BlockSpec(memory_space=pltpu.VMEM)
    hbm = pl.BlockSpec(memory_space=pl.ANY)
    dma = pltpu.SemaphoreType.DMA
    return pl.pallas_call(
        functools.partial(kernel, size_x, size_y),
        out_shape=jax.ShapeDtypeStruct((rows, cols), jnp.float32),
        in_specs=[pl.BlockSpec(memory_space=pltpu.SMEM), vmem, vmem, hbm, hbm] + [vmem] * 4,
        out_specs=vmem,
        scratch_shapes=[
            pltpu.VMEM((rows, cols), jnp.float32),
            pltpu.VMEM((3, frame, cols + 128), jnp.float32),
            pltpu.VMEM((frame, cols + 128), jnp.float32),
            pltpu.VMEM((size_x, 8, cols), jnp.float32),
            pltpu.VMEM((size_y, 8, rows), jnp.float32),
            pltpu.VMEM((3, 2, HALO, frame), jnp.float32),
            pltpu.VMEM((3, 2, HALO, frame), jnp.float32),
            dma((3,)),
            dma((size_x,)),
            dma((size_x,)),
            dma((size_y,)),
            dma((size_y,)),
            dma((3, 2)),
            dma((3, 2)),
            dma((3, 2)),
            dma((3, 2)),
        ],
        compiler_params=pltpu.CompilerParams(
            collective_id=0, has_side_effects=True, vmem_limit_bytes=50 * 2**20
        ),
        name="restart",
    )(*operands)


def tile_weights(grid_levels, coefficients, faulty_grids, shape):
    grid_ids = jnp.arange(coefficients.shape[0], dtype=jnp.int32)
    alive = jnp.all(faulty_grids[None, :] != grid_ids[:, None], axis=1)
    share = jnp.where(alive, coefficients, 0).astype(jnp.float32)
    masks = jnp.left_shift(1, grid_levels) - 1
    row = jnp.arange(shape[0], dtype=jnp.int32)
    col = jnp.arange(shape[1], dtype=jnp.int32)
    on_row = (row[None, :] & masks[:, 0:1]) == 0
    on_col = (col[None, :] & masks[:, 1:2]) == 0
    return jnp.sum(
        jnp.where(on_row[:, :, None] & on_col[:, None, :], share[:, None, None], 0.0), axis=0
    )


def local(
    owned_surplus, tile_owner, grid_levels, coefficients, faulty_grids, velocity_x, velocity_y
):
    slot_count, tile_height, tile_width = owned_surplus.shape
    size_x = lax.axis_size("gx")
    size_y = lax.axis_size("gy")
    device_count = size_x * size_y
    capacity = 2 * slot_count // device_count
    own_index = lax.axis_index("gx") * size_y + lax.axis_index("gy")
    offsets = tile_owner[:slot_count]
    positions = jnp.arange(slot_count, dtype=jnp.int32)
    same_offset = offsets[:, None] == offsets[None, :]
    earlier = positions[None, :] < positions[:, None]
    slot_rank = jnp.sum((same_offset & earlier).astype(jnp.int32), axis=1)
    target = (own_index - offsets) % device_count
    seat = target * capacity + slot_rank
    seats = jnp.arange(device_count * capacity, dtype=jnp.int32)
    holder = jnp.max(jnp.where(seat[None, :] == seats[:, None], positions[None, :], 0), axis=1)
    outgoing = jnp.take(owned_surplus, holder, axis=0, mode="clip")
    incoming = lax.all_to_all(
        outgoing.reshape(device_count, capacity, tile_height, tile_width),
        ("gx", "gy"),
        split_axis=0,
        concat_axis=0,
        tiled=True,
    )
    incoming = incoming.reshape(device_count * capacity, tile_height, tile_width)
    place = (own_index + offsets) % device_count * capacity + slot_rank
    weight = tile_weights(grid_levels, coefficients, faulty_grids, (tile_height, tile_width))
    return restart(place, weight, incoming, velocity_x, velocity_y, size_x, size_y)


def solution(mesh):
    return jax.shard_map(
        local,
        mesh=mesh,
        in_specs=(P(("gx", "gy"), None, None), P(), P(), P(), P(), P("gx", "gy"), P("gx", "gy")),
        out_specs=P("gx", "gy"),
        check_vma=False,
    )
```

time: 331 us -> 169 us (0.51)
  other arithmetic: 64.8 us -> 1.33 us
  waiting for transfers between devices: 157 us -> 94.8 us
  Pallas kernels: 0 us -> 59.7 us
  local copies, waits for them, and re-layouts: 50.3 us -> 5.21 us
  blocking collectives: 31.2 us -> 0 us
  starting transfers between devices: 23.5 us -> 7.43 us
    ppermute x16 -> x0, waiting for transfers between devices: 63.3 us -> none  [the longest x8 58.7 us: padded_2(): before = lax.ppermute(last, axis, up)]
    pallas_call x0 -> x1, Pallas kernels: none -> 59.7 us  [restart(): pl.pallas_call(functools.partial(kernel, size_x, size_y), out_shape=jax.S...]
    scatter x20 -> x0, other arithmetic: 32.9 us -> none  [refine(): values.at[spacing::2 * spacing]]
    all_gather x2 -> x0, blocking collectives: 31.2 us -> none  [the longest x1 26 us: local(): skeleton_y = lax.all_gather(nodal_x[:, 0:1], 'gy', axis=1, tiled=True).T]
    scatter x8 -> x0, local copies, waits for them, and re-layouts: 18.1 us -> none  [the longest x1 15.7 us: local(): outgoing = outgoing.at[target * capacity + slot_rank].set(owned_surplus)]
    ppermute x16 -> x0, starting transfers between devices: 16.1 us -> none  [the longest x8 9.76 us: padded_2(): after = lax.ppermute(initial, axis, down)]
    slice x47 -> x1, local copies, waits for them, and re-layouts: 14.2 us -> 0.01 us  [tile_weights(): on_row = row[None, :] & masks[:, 0:1] == 0]
    mul x2 -> x0, other arithmetic: 11.6 us -> none  [local(): field_now = 0.5 * (field_now + middle_field + TIME_STEP * second_rate)]
  transfers between devices with their start and end apart: 17 -> 1, of which waited for: 11 -> 1; matrix products, arithmetic and copies ran while one was open for 2% -> 0% of each run, Pallas kernels for 0% -> 0%
where the time goes in v1:
time: 169 us
  waiting for transfers between devices  94.8 us (56%)
  Pallas kernels  59.7 us (35%)
  starting transfers between devices  7.43 us (4%)
  local copies, waits for them, and re-layouts  5.21 us (3%)
    all_to_all x1, waiting for transfers between devices, local(): lax.all_to_all(outgoing.reshape(device_count, capacity, tile_height, tile...  94.8 us
    pallas_call x1, Pallas kernels, restart(): pl.pallas_call(functools.partial(kernel, size_x, size_y), out_shape=jax.S...  59.7 us
    all_to_all x1, starting transfers between devices, local(): lax.all_to_all(outgoing.reshape(device_count, capacity, tile_height, tile...  7.43 us
  transfers between devices with their start and end apart: 1, of which 1 were waited for; matrix products, arithmetic and copies ran while one was open for 0% of the time, Pallas kernels for 0%

profile of v1, /device:TPU:0, one launch (start us, length us, event | category | flops | bytes accessed | tf_op | source)
XLA Modules:
  0.0 168.6 jit_solution(10869046616875751148)
XLA Ops:
  0.0 0.0 copy-start
  0.0 0.8 slice.11
  0.8 0.2 convert_reduce_fusion
  1.0 0.7 fusion.4
  1.7 0.1 select_reduce_fusion
  1.9 0.0 copy-done
  1.9 3.0 %gather_fusion = f32[256,16,256]{2,1,0:T(8,128)} fusion(f32[128,16,256]{2,1,0:T(8,128)S(1)} %copy-done, s32[1024]{0:T(1024)S(1)} %pad_clamp_fusion), kind=kCustom, calls=%fused_computation | custom fusion | bytes 8389632 | tf_op jit(solution)/shard_map/jit(_take)/gather | solution.py:412
  4.9 0.0 copy-start.6
  4.9 0.0 copy-start.5
  4.9 0.0 copy-start.7
  4.9 0.0 copy-start.1
  4.9 0.0 copy-start.2
  4.9 0.0 copy-start.3
  4.9 0.0 copy-start.4
  4.9 7.4 %all-to-all-start = ((f32[32,8,16,256]{3,2,1,0:T(8,128)}), f32[32,8,16,256]{3,2,1,0:T(8,128)}, u32[]{:S(2)}, u32[]{:S(2)}) async-start(f32[32,8,16,256]{3,2,1,0:T(8,128)} %bitcast.6), calls=%async_computation | async-start | bytes 8388608 | tf_op jit(solution)/shard_map/all_to_all | solution.py:413
  12.4 0.0 copy-done.6
  12.4 0.1 compare_reduce_fusion
  12.5 0.0 copy-done.5
  12.5 0.1 and_compare_fusion.1
  12.6 0.0 copy-done.7
  12.6 0.1 and_compare_fusion
  12.6 0.1 select_reduce_fusion.1.weight_ref
  12.7 94.8 %all-to-all-done = f32[32,8,16,256]{3,2,1,0:T(8,128)} async-done(((f32[32,8,16,256]{3,2,1,0:T(8,128)}), f32[32,8,16,256]{3,2,1,0:T(8,128)}, u32[]{:S(2)}, u32[]{:S(2)}) %all-to-all-start) | async-done | bytes 4194336 | tf_op jit(solution)/shard_map/all_to_all | solution.py:413
  107.5 0.0 copy-done.1
  107.5 0.0 copy-done.2
  107.5 0.0 copy-done.3
  107.5 0.0 copy-done.4
  107.5 59.7 %restart.1 = f32[512,1024]{1,0:T(8,128)S(1)} custom-call(s32[128]{0:T(128)S(1)} %get-tuple-element.6.place_ref, f32[16,256]{1,0:T(8,128)S(1)} %select_reduce_fusion.1.weight_ref, f32[256,16,256]{2,1,0:T(8,128)} %bitcast.3.incoming_ref, f32[512,1024]{1,0:T(8,128)} %vel_x_ref.1, f32[512,1024]{1,0:T(8,128)} %vel_y_ref.1, bf16[256,256]{1,0:T(8,128)(2,1)S(1)} %copy-done.1, ...), custom_call_target="tpu_custom_call" | custom-call | tf_op jit(solution)/shard_map/restart/pallas_call | solution.py:350
  167.2 1.3 copy.13
  (4 shorter events, 0.0 us)
Async XLA Ops:
  0.0 1.9 %copy-start = (f32[128,16,256]{2,1,0:T(8,128)S(1)}, f32[128,16,256]{2,1,0:T(8,128)}, u32[]{:S(2)}) copy-start(f32[128,16,256]{2,1,0:T(8,128)} %param.11) | copy-start | bytes 6291460
  4.9 7.5 %copy-start.6 = (s32[2]{0:T(128)S(1)}, s32[2]{0:T(128)}, u32[]{:S(2)}) copy-start(s32[2]{0:T(128)} %param.15) | copy-start | bytes 28
  4.9 7.6 %copy-start.5 = (s32[8,2]{0,1:T(2,128)S(1)}, s32[8,2]{0,1:T(2,128)}, u32[]{:S(2)}) copy-start(s32[8,2]{0,1:T(2,128)} %param.13) | copy-start | bytes 196
  4.9 7.7 %copy-start.7 = (s32[8]{0:T(128)S(1)}, s32[8]{0:T(128)}, u32[]{:S(2)}) copy-start(s32[8]{0:T(128)} %param.14) | copy-start | bytes 100
  4.9 102.6 %copy-start.1 = (bf16[256,256]{1,0:T(8,128)(2,1)S(1)}, bf16[256,256]{1,0:T(8,128)(2,1)}, u32[]{:S(2)}) copy-start(bf16[256,256]{1,0:T(8,128)(2,1)} %constant.52.clone.hats_ref) | copy-start | bytes 393220
  4.9 102.6 %copy-start.2 = (bf16[256,256]{1,0:T(8,128)(2,1)S(1)}, bf16[256,256]{1,0:T(8,128)(2,1)}, u32[]{:S(2)}) copy-start(bf16[256,256]{1,0:T(8,128)(2,1)} %constant.53.clone.hats_t_ref) | copy-start | bytes 393220
  4.9 102.6 %copy-start.3 = (f32[8,8,64]{2,1,0:T(8,128)S(1)}, f32[8,8,64]{2,1,0:T(8,128)}, u32[]{:S(2)}) copy-start(f32[8,8,64]{2,1,0:T(8,128)} %constant.55.clone.coarse_y_ref) | copy-start | bytes 49156
  4.9 102.6 %copy-start.4 = (f32[4,8,32]{2,1,0:T(8,128)S(1)}, f32[4,8,32]{2,1,0:T(8,128)}, u32[]{:S(2)}) copy-start(f32[4,8,32]{2,1,0:T(8,128)} %constant.54.clone.coarse_x_ref) | copy-start | bytes 12292
  4.9 102.6 %all-to-all-start = ((f32[32,8,16,256]{3,2,1,0:T(8,128)}), f32[32,8,16,256]{3,2,1,0:T(8,128)}, u32[]{:S(2)}, u32[]{:S(2)}) async-start(f32[32,8,16,256]{3,2,1,0:T(8,128)} %bitcast.6), calls=%async_computation | async-start | bytes 8388608 | tf_op jit(solution)/shard_map/all_to_all | solution.py:413

commit v2 on v1

v2 whole, which is shorter than its diff:
```python
import functools

import jax
import jax.numpy as jnp
import ml_dtypes
import numpy as np
from jax import lax
from jax.experimental import pallas as pl
from jax.experimental.pallas import tpu as pltpu
from jax.sharding import PartitionSpec as P

STEPS = 2
TIME_STEP = 0.2
CHUNK = 256
HALO = 8
TOP = 16
MESH = pl.DeviceIdType.MESH


def hat_matrix():
    points = np.arange(CHUNK)[:, None]
    nodes = np.arange(CHUNK)[None, :]
    reach = np.where(nodes == 0, 1, nodes & -nodes)
    hats = np.maximum(0.0, 1.0 - np.abs(points - nodes) / reach)
    hats[:, 0] = 0.0
    return hats


def coarse_matrix(count):
    values = np.eye(count)
    spacing = count // 2
    while spacing >= 1:
        for x in range(spacing, count, 2 * spacing):
            values[x] += 0.5 * (values[x - spacing] + values[(x + spacing) % count])
        spacing //= 2
    return values


FIRST = tuple(range(1, 9)) + (16, 32, 64, 128)
LAST = (128, 192, 224, 240) + tuple(range(248, 256))
PACK = 16


def frame_table(size, per_device, length, corner_row, right_row, left_row):
    total = size * per_device
    full = coarse_matrix(total)
    hats = hat_matrix()
    table = np.zeros((size, length, size * 8 + 2 * PACK))
    spots = np.array([(j // per_device) * 8 + j % per_device for j in range(total)])
    for me in range(size):
        for c in range(per_device + 1):
            table[me, corner_row + c, spots] = full[(me * per_device + c) % total]
        for k in range(HALO):
            for row, chunk, point, nodes, start in (
                (right_row + k, (me + 1) * per_device, k, FIRST, size * 8),
                (left_row + k, me * per_device - 1, CHUNK - HALO + k, LAST, size * 8 + PACK),
            ):
                part = point / CHUNK
                table[me, row, spots] = (1 - part) * full[chunk % total] + part * full[
                    (chunk + 1) % total
                ]
                for i, node in enumerate(nodes):
                    table[me, row, start + i] = hats[point, node]
    return table.astype(np.float32)


def split_dot(matrix, values, left):
    high = values.astype(jnp.bfloat16)
    low = (values - high.astype(jnp.float32)).astype(jnp.bfloat16)
    if left:
        return jnp.dot(matrix, high, preferred_element_type=jnp.float32) + jnp.dot(
            matrix, low, preferred_element_type=jnp.float32
        )
    return jnp.dot(high, matrix, preferred_element_type=jnp.float32) + jnp.dot(
        low, matrix, preferred_element_type=jnp.float32
    )


def exact_dot(a, b):
    return jnp.dot(a, b, precision=lax.Precision.HIGHEST, preferred_element_type=jnp.float32)


def kernel(
    size_x,
    size_y,
    place_ref,
    weight_ref,
    outgoing_ref,
    vel_x_ref,
    vel_y_ref,
    hats_ref,
    hats_t_ref,
    table_x_ref,
    table_y_ref,
    out_ref,
    incoming,
    block,
    field,
    middle,
    later,
    vel_x,
    vel_y,
    rows_all,
    row_send,
    row_recv,
    cols_all,
    col_send,
    col_recv,
    side_send,
    side_recv,
    local_sem,
    tile_send_sem,
    tile_recv_sem,
    rows_sem,
    row_pack_sem,
    cols_sem,
    col_pack_sem,
    face_sem,
    side_sem,
):
    rows, cols = out_ref.shape
    tile_rows, tile_cols = weight_ref.shape
    across = cols // tile_cols
    devices = size_x * size_y
    capacity = incoming.shape[0] // devices
    frame = block.shape[0]
    chunks_x = rows // CHUNK
    chunks_y = cols // CHUNK
    ix = lax.axis_index("gx")
    iy = lax.axis_index("gy")
    me = ix * size_y + iy
    before_x = (lax.rem(ix + size_x - 1, size_x), iy)
    after_x = (lax.rem(ix + 1, size_x), iy)
    before_y = (ix, lax.rem(iy + size_y - 1, size_y))
    after_y = (ix, lax.rem(iy + 1, size_y))

    def remote(src, dst, send_sem, recv_sem, device):
        return pltpu.make_async_remote_copy(
            src_ref=src,
            dst_ref=dst,
            send_sem=send_sem,
            recv_sem=recv_sem,
            device_id=device,
            device_id_type=MESH,
        )

    def partner(step):
        other = lax.rem(me + step, devices)
        return (other // size_y, lax.rem(other, size_y))

    own_tiles = pl.ds(pl.multiple_of(me * capacity, capacity), capacity)
    loads = [
        pltpu.make_async_copy(
            source, target.at[pl.ds(TOP, rows), pl.ds(0, cols)], local_sem.at[f]
        )
        for f, source, target in ((0, vel_x_ref, vel_x), (1, vel_y_ref, vel_y))
    ]
    loads.append(
        pltpu.make_async_copy(outgoing_ref.at[own_tiles], incoming.at[own_tiles], local_sem.at[2])
    )
    for load in loads:
        load.start()

    barrier = pltpu.get_barrier_semaphore()

    def greet(step, carry):
        pl.semaphore_signal(barrier, inc=1, device_id=partner(step), device_id_type=MESH)
        return carry

    lax.fori_loop(1, devices, greet, 0)
    pl.semaphore_wait(barrier, devices - 1)

    def tile_copy(step):
        other = lax.rem(me + step, devices)
        return remote(
            outgoing_ref.at[pl.ds(pl.multiple_of(other * capacity, capacity), capacity)],
            incoming.at[own_tiles],
            tile_send_sem.at[step],
            tile_recv_sem.at[step],
            partner(step),
        )

    for load in loads[:2]:
        load.wait()
    face_copies = [
        remote(
            vel.at[pl.ds(start, HALO), pl.ds(0, cols)],
            vel.at[pl.ds(target, HALO), pl.ds(0, cols)],
            face_sem.at[f, side, 0],
            face_sem.at[f, side, 1],
            device,
        )
        for f, vel in enumerate((vel_x, vel_y))
        for side, start, target, device in (
            (0, TOP, TOP + rows, before_x),
            (1, TOP + rows - HALO, TOP - HALO, after_x),
        )
    ]
    for copy in face_copies:
        copy.start()

    def send_tiles(step, carry):
        tile_copy(step).start()
        return carry

    lax.fori_loop(1, devices, send_tiles, 0)

    for copy in face_copies:
        copy.wait()
    side_copies = []
    for f, vel in enumerate((vel_x, vel_y)):
        side_send[f, 0] = vel[:, 0:128].T[0:HALO]
        side_send[f, 1] = vel[:, cols - 128 : cols].T[128 - HALO : 128]
        for side, device in ((0, before_y), (1, after_y)):
            side_copies.append(
                remote(
                    side_send.at[f, side],
                    side_recv.at[f, side],
                    side_sem.at[f, side, 0],
                    side_sem.at[f, side, 1],
                    device,
                )
            )
    for copy in side_copies:
        copy.start()
    for copy in side_copies:
        copy.wait()
    for f, vel in enumerate((vel_x, vel_y)):
        strip = jnp.concatenate(
            [
                side_recv[f, 0],
                jnp.zeros((128 - 2 * HALO, frame), jnp.float32),
                side_recv[f, 1],
            ],
            axis=0,
        )
        vel[:, cols : cols + 128] = strip.T

    loads[2].wait()

    def receive_tiles(step, carry):
        tile_copy(step).wait()
        return carry

    lax.fori_loop(1, devices, receive_tiles, 0)

    weight = weight_ref[...]

    def put(kx, carry):
        start = pl.multiple_of(TOP + kx * tile_rows, tile_rows)
        for ky in range(across):
            block[pl.ds(start, tile_rows), ky * tile_cols : (ky + 1) * tile_cols] = (
                incoming[place_ref[kx * across + ky]] * weight
            )
        return carry

    lax.fori_loop(0, rows // tile_rows, put, 0, unroll=2)

    def row(point):
        return block[TOP + point : TOP + point + 1, :]

    def pack_rows(start, nodes):
        return jnp.concatenate(
            [row(start + node) for node in nodes]
            + [jnp.zeros((PACK - len(nodes), cols), jnp.float32)],
            axis=0,
        )

    rows_all[ix] = jnp.concatenate(
        [row(c * CHUNK) for c in range(chunks_x)]
        + [jnp.zeros((8 - chunks_x, cols), jnp.float32)],
        axis=0,
    )
    row_send[0] = pack_rows(0, FIRST)
    row_send[1] = pack_rows(rows - CHUNK, LAST)
    row_copies = [
        remote(
            rows_all.at[ix],
            rows_all.at[ix],
            rows_sem.at[step, 0],
            rows_sem.at[step, 1],
            (lax.rem(ix + step, size_x), iy),
        )
        for step in range(1, size_x)
    ] + [
        remote(
            row_send.at[side],
            row_recv.at[side],
            row_pack_sem.at[side, 0],
            row_pack_sem.at[side, 1],
            device,
        )
        for side, device in ((0, before_x), (1, after_x))
    ]
    for copy in row_copies:
        copy.start()

    for c in range(chunks_x):
        span = slice(TOP + c * CHUNK, TOP + (c + 1) * CHUNK)
        block[span, :] = split_dot(hats_ref[...], block[span, :], True)

    for copy in row_copies:
        copy.wait()
    known = jnp.concatenate(
        [rows_all[...].reshape(size_x * 8, cols), row_recv[...].reshape(2 * PACK, cols)], axis=0
    )
    ends = exact_dot(table_x_ref[ix], known)
    part = lax.broadcasted_iota(jnp.int32, (CHUNK, 1), 0).astype(jnp.float32) * (1.0 / CHUNK)
    for c in range(chunks_x):
        span = slice(TOP + c * CHUNK, TOP + (c + 1) * CHUNK)
        block[span, :] += (1.0 - part) * ends[c : c + 1] + part * ends[c + 1 : c + 2]
    block[TOP + rows : TOP + rows + HALO, :] = ends[8:16]
    block[TOP - HALO : TOP, :] = ends[16:24]

    lane = lax.broadcasted_iota(jnp.int32, (frame, 128), 1)
    picked = block[:, 0:128]
    for spot, point in enumerate([128] + [c * CHUNK for c in range(1, chunks_y)]):
        picked = jnp.where(lane == 10 + spot, block[:, point : point + 1], picked)
    first = picked.T
    last_cols = block[:, cols - 128 : cols].T
    blank = jnp.zeros((8, frame), jnp.float32)
    cols_all[iy] = jnp.concatenate(
        [first[0:1], first[11 : 10 + chunks_y], blank[: 8 - chunks_y]], axis=0
    )
    col_send[0] = jnp.concatenate(
        [first[1:9], first[16:17], first[32:33], first[64:65], first[10:11], blank[:4]], axis=0
    )
    col_send[1] = jnp.concatenate(
        [last_cols[node - 128 : node - 127] for node in LAST] + [blank[:4]], axis=0
    )
    col_copies = [
        remote(
            cols_all.at[iy],
            cols_all.at[iy],
            cols_sem.at[step, 0],
            cols_sem.at[step, 1],
            (ix, lax.rem(iy + step, size_y)),
        )
        for step in range(1, size_y)
    ] + [
        remote(
            col_send.at[side],
            col_recv.at[side],
            col_pack_sem.at[side, 0],
            col_pack_sem.at[side, 1],
            device,
        )
        for side, device in ((0, before_y), (1, after_y))
    ]
    for copy in col_copies:
        copy.start()

    used = rows + 2 * TOP
    for c in range(chunks_y):
        span = slice(c * CHUNK, (c + 1) * CHUNK)
        block[0:used, span] = split_dot(hats_t_ref[...], block[0:used, span], False)

    for copy in col_copies:
        copy.wait()
    known = jnp.concatenate(
        [cols_all[...].reshape(size_y * 8, frame), col_recv[...].reshape(2 * PACK, frame)], axis=0
    )
    ends = exact_dot(table_y_ref[iy], known).T
    field[:, cols : cols + 128] = ends
    part = lax.broadcasted_iota(jnp.int32, (1, CHUNK), 1).astype(jnp.float32) * (1.0 / CHUNK)
    for c in range(chunks_y):
        span = slice(c * CHUNK, (c + 1) * CHUNK)
        field[0:used, span] = (
            block[0:used, span]
            + (1.0 - part) * ends[0:used, 8 + c : 9 + c]
            + part * ends[0:used, 9 + c : 10 + c]
        )

    width = cols + 128
    scale = TIME_STEP / 12.0

    def change(ref, start):
        around = ref.at[pl.ds(pl.multiple_of(start - 8, 8), 24), :]

        def read(shift):
            return around[8 + shift : 16 + shift, :]

        centre = read(0)
        west_one, east_one = read(-1), read(1)
        west_two, east_two = read(-2), read(2)
        north_one = pltpu.roll(centre, width - 1, 1)
        south_one = pltpu.roll(centre, 1, 1)
        north_two = pltpu.roll(centre, width - 2, 1)
        south_two = pltpu.roll(centre, 2, 1)
        near = (east_one + west_one) + (north_one + south_one)
        far = (east_two + west_two) + (north_two + south_two)
        slope_x = 8.0 * (east_one - west_one) - (east_two - west_two)
        slope_y = 8.0 * (north_one - south_one) - (north_two - south_two)
        total = (8.0 * near - 0.5 * far - 30.0 * centre) - (
            vel_x[pl.ds(start, 8), :] * slope_x + vel_y[pl.ds(start, 8), :] * slope_y
        )
        return centre, scale * total

    def sweep(start, count, body):
        def strip(i, carry):
            body(pl.multiple_of(start + i * 8, 8))
            return carry

        group = next(g for g in (8, 6, 4, 3, 2, 1) if count % g == 0)
        lax.fori_loop(0, count, strip, 0, unroll=group)

    now, then = field, later
    for step in range(STEPS):
        last = step == STEPS - 1

        def first_half(start, now=now):
            centre, delta = change(now, start)
            middle[pl.ds(start, 8), :] = centre + delta

        def second_half(start, now=now, then=then, last=last):
            centre, delta = change(middle, start)
            value = 0.5 * (now[pl.ds(start, 8), :] + centre + delta)
            if last:
                out_ref[pl.ds(pl.multiple_of(start - TOP, 8), 8), :] = value[:, :cols]
            else:
                then[pl.ds(start, 8), :] = value

        sweep(TOP - HALO, (rows + 2 * HALO) // 8, first_half)
        if last:
            sweep(TOP, rows // 8, second_half)
        else:
            sweep(TOP - HALO, (rows + 2 * HALO) // 8, second_half)
        now, then = then, now


def restart(place, weight, outgoing, vel_x, vel_y, size_x, size_y):
    rows, cols = vel_x.shape
    frame = (rows + 2 * TOP + 127) // 128 * 128
    devices = size_x * size_y
    hats = hat_matrix()
    operands = (
        place,
        weight,
        outgoing,
        vel_x,
        vel_y,
        jnp.asarray(hats.astype(ml_dtypes.bfloat16)),
        jnp.asarray(hats.T.astype(ml_dtypes.bfloat16)),
        jnp.asarray(frame_table(size_x, rows // CHUNK, 24, 0, 8, 16)),
        jnp.asarray(frame_table(size_y, cols // CHUNK, 128, 8, 0, 120)),
    )
    vmem = pl.BlockSpec(memory_space=pltpu.VMEM)
    hbm = pl.BlockSpec(memory_space=pl.ANY)
    dma = pltpu.SemaphoreType.DMA
    framed = pltpu.VMEM((frame, cols + 128), jnp.float32)
    return pl.pallas_call(
        functools.partial(kernel, size_x, size_y),
        out_shape=jax.ShapeDtypeStruct((rows, cols), jnp.float32),
        in_specs=[pl.BlockSpec(memory_space=pltpu.SMEM), vmem, hbm, hbm, hbm] + [vmem] * 4,
        out_specs=vmem,
        scratch_shapes=[
            pltpu.VMEM(outgoing.shape, jnp.float32),
            pltpu.VMEM((frame, cols), jnp.float32),
            framed,
            framed,
            framed,
            framed,
            framed,
            pltpu.VMEM((size_x, 8, cols), jnp.float32),
            pltpu.VMEM((2, PACK, cols), jnp.float32),
            pltpu.VMEM((2, PACK, cols), jnp.float32),
            pltpu.VMEM((size_y, 8, frame), jnp.float32),
            pltpu.VMEM((2, PACK, frame), jnp.float32),
            pltpu.VMEM((2, PACK, frame), jnp.float32),
            pltpu.VMEM((2, 2, HALO, frame), jnp.float32),
            pltpu.VMEM((2, 2, HALO, frame), jnp.float32),
            dma((3,)),
            dma((devices,)),
            dma((devices,)),
            dma((size_x, 2)),
            dma((2, 2)),
            dma((size_y, 2)),
            dma((2, 2)),
            dma((2, 2, 2)),
            dma((2, 2, 2)),
        ],
        compiler_params=pltpu.CompilerParams(
            collective_id=0, has_side_effects=True, vmem_limit_bytes=50 * 2**20
        ),
        name="restart",
    )(*operands)


def tile_weights(grid_levels, coefficients, faulty_grids, shape):
    grid_ids = jnp.arange(coefficients.shape[0], dtype=jnp.int32)
    alive = jnp.all(faulty_grids[None, :] != grid_ids[:, None], axis=1)
    share = jnp.where(alive, coefficients, 0).astype(jnp.float32)
    masks = jnp.left_shift(1, grid_levels) - 1
    row = jnp.arange(shape[0], dtype=jnp.int32)
    col = jnp.arange(shape[1], dtype=jnp.int32)
    on_row = (row[None, :] & masks[:, 0:1]) == 0
    on_col = (col[None, :] & masks[:, 1:2]) == 0
    return jnp.sum(
        jnp.where(on_row[:, :, None] & on_col[:, None, :], share[:, None, None], 0.0), axis=0
    )


def local(
    owned_surplus, tile_owner, grid_levels, coefficients, faulty_grids, velocity_x, velocity_y
):
    slot_count, tile_height, tile_width = owned_surplus.shape
    size_x = lax.axis_size("gx")
    size_y = lax.axis_size("gy")
    device_count = size_x * size_y
    capacity = 2 * slot_count // device_count
    own_index = lax.axis_index("gx") * size_y + lax.axis_index("gy")
    offsets = tile_owner[:slot_count]
    positions = jnp.arange(slot_count, dtype=jnp.int32)
    same_offset = offsets[:, None] == offsets[None, :]
    earlier = positions[None, :] < positions[:, None]
    slot_rank = jnp.sum((same_offset & earlier).astype(jnp.int32), axis=1)
    target = (own_index - offsets) % device_count
    seat = target * capacity + slot_rank
    seats = jnp.arange(device_count * capacity, dtype=jnp.int32)
    holder = jnp.max(jnp.where(seat[None, :] == seats[:, None], positions[None, :], 0), axis=1)
    outgoing = jnp.take(owned_surplus, holder, axis=0, mode="clip")
    place = (own_index + offsets) % device_count * capacity + slot_rank
    weight = tile_weights(grid_levels, coefficients, faulty_grids, (tile_height, tile_width))
    return restart(place, weight, outgoing, velocity_x, velocity_y, size_x, size_y)


def solution(mesh):
    return jax.shard_map(
        local,
        mesh=mesh,
        in_specs=(P(("gx", "gy"), None, None), P(), P(), P(), P(), P("gx", "gy"), P("gx", "gy")),
        out_specs=P("gx", "gy"),
        check_vma=False,
    )
```

time: 169 us -> 148 us (0.88)
  waiting for transfers between devices: 94.8 us -> 0 us
  Pallas kernels: 59.7 us -> 139 us
  starting transfers between devices: 7.43 us -> 0 us
  other arithmetic: 1.33 us -> 3.47 us
    all_to_all x1 -> x0, waiting for transfers between devices: 94.8 us -> none  [local(): lax.all_to_all(outgoing.reshape(device_count, capacity, tile_height, tile...]
    pallas_call x1, Pallas kernels: 59.7 us -> 139 us  [restart(): pl.pallas_call(functools.partial(kernel, size_x, size_y), out_shape=jax.S...]
    all_to_all x1 -> x0, starting transfers between devices: 7.43 us -> none  [local(): lax.all_to_all(outgoing.reshape(device_count, capacity, tile_height, tile...]
  transfers between devices with their start and end apart: 1 -> 0, of which waited for: 1 -> 0; matrix products, arithmetic and copies ran while one was open for 0% -> 0% of each run, Pallas kernels for 0% -> 0%
where the time goes in v2:
time: 148 us
  Pallas kernels  139 us (94%)
  local copies, waits for them, and re-layouts  5.02 us (3%)
  other arithmetic  3.47 us (2%)
    pallas_call x1, Pallas kernels, restart(): pl.pallas_call(functools.partial(kernel, size_x, size_y), out_shape=jax.S...  139 us
    gather x1, local copies, waits for them, and re-layouts, local(): outgoing = jnp.take(owned_surplus, holder, axis=0, mode='clip')  2.97 us

profile of v2, /device:TPU:0, one launch (start us, length us, event | category | flops | bytes accessed | tf_op | source)
XLA Modules:
  0.0 147.8 jit_solution(4613235646837989960)
XLA Ops:
  0.0 0.0 copy-start
  0.0 0.9 compare_reduce_fusion
  0.9 0.7 select_convert_fusion
  1.6 0.7 slice.11
  2.2 0.2 convert_reduce_fusion
  2.4 0.7 fusion.4
  3.1 0.1 select_reduce_fusion
  3.2 0.7 shift-left_add_fusion
  3.9 0.1 and_compare_fusion.1
  4.0 0.1 and_compare_fusion
  4.1 0.1 select_reduce_fusion.1.weight_ref
  4.2 0.0 copy-done
  4.2 0.0 copy-start.1
  4.2 0.0 copy-start.2
  4.2 0.0 copy-start.3
  4.2 0.0 copy-start.4
  4.2 3.0 %gather_fusion = f32[256,16,256]{2,1,0:T(8,128)} fusion(f32[128,16,256]{2,1,0:T(8,128)S(1)} %copy-done, s32[1024]{0:T(1024)S(1)} %pad_clamp_fusion), kind=kCustom, calls=%fused_computation | custom fusion | bytes 8389632 | tf_op jit(solution)/shard_map/jit(_take)/gather | solution.py:521
  7.2 0.0 copy-done.1
  7.2 0.0 copy-done.2
  7.2 0.0 copy-done.3
  7.2 0.0 copy-done.4
  7.2 139.3 %restart.1 = f32[512,1024]{1,0:T(8,128)S(1)} custom-call(s32[128]{0:T(128)S(1)} %get-tuple-element.6.place_ref, f32[16,256]{1,0:T(8,128)S(1)} %select_reduce_fusion.1.weight_ref, f32[256,16,256]{2,1,0:T(8,128)} %gather_fusion, f32[512,1024]{1,0:T(8,128)} %vel_x_ref.1, f32[512,1024]{1,0:T(8,128)} %vel_y_ref.1, bf16[256,256]{1,0:T(8,128)(2,1)S(1)} %copy-done.3, ...), custom_call_target="tpu_custom_call" | custom-call | tf_op jit(solution)/shard_map/restart/pallas_call | solution.py:451
  146.5 1.3 copy.13
  (2 shorter events, 0.0 us)
Async XLA Ops:
  0.0 4.2 %copy-start = (f32[128,16,256]{2,1,0:T(8,128)S(1)}, f32[128,16,256]{2,1,0:T(8,128)}, u32[]{:S(2)}) copy-start(f32[128,16,256]{2,1,0:T(8,128)} %param.11) | copy-start | bytes 6291460
  4.2 3.0 %copy-start.1 = (f32[8,128,96]{2,1,0:T(8,128)S(1)}, f32[8,128,96]{2,1,0:T(8,128)}, u32[]{:S(2)}) copy-start(f32[8,128,96]{2,1,0:T(8,128)} %constant.55.clone.table_y_ref) | copy-start | bytes 1179652
  4.2 3.0 %copy-start.2 = (bf16[256,256]{1,0:T(8,128)(2,1)S(1)}, bf16[256,256]{1,0:T(8,128)(2,1)}, u32[]{:S(2)}) copy-start(bf16[256,256]{1,0:T(8,128)(2,1)} %constant.53.clone.hats_t_ref) | copy-start | bytes 393220
  4.2 3.0 %copy-start.3 = (bf16[256,256]{1,0:T(8,128)(2,1)S(1)}, bf16[256,256]{1,0:T(8,128)(2,1)}, u32[]{:S(2)}) copy-start(bf16[256,256]{1,0:T(8,128)(2,1)} %constant.52.clone.hats_ref) | copy-start | bytes 393220
  4.2 3.0 %copy-start.4 = (f32[4,24,64]{2,1,0:T(8,128)S(1)}, f32[4,24,64]{2,1,0:T(8,128)}, u32[]{:S(2)}) copy-start(f32[4,24,64]{2,1,0:T(8,128)} %constant.54.clone.table_x_ref) | copy-start | bytes 73732

commit v3 on v2

--- a/solution.py
+++ b/solution.py
@@ -83,9 +83,13 @@
 def kernel(
     size_x,
     size_y,
-    place_ref,
-    weight_ref,
-    outgoing_ref,
+    owner_ref,
+    rank_ref,
+    holder_ref,
+    levels_ref,
+    coefficients_ref,
+    faulty_ref,
+    owned_ref,
     vel_x_ref,
     vel_y_ref,
     hats_ref,
@@ -93,6 +97,7 @@
     table_x_ref,
     table_y_ref,
     out_ref,
+    outgoing,
     incoming,
     block,
     field,
@@ -119,7 +124,7 @@
     side_sem,
 ):
     rows, cols = out_ref.shape
-    tile_rows, tile_cols = weight_ref.shape
+    _, tile_rows, tile_cols = owned_ref.shape
     across = cols // tile_cols
     devices = size_x * size_y
     capacity = incoming.shape[0] // devices
@@ -148,16 +153,12 @@
         other = lax.rem(me + step, devices)
         return (other // size_y, lax.rem(other, size_y))
 
-    own_tiles = pl.ds(pl.multiple_of(me * capacity, capacity), capacity)
     loads = [
         pltpu.make_async_copy(
             source, target.at[pl.ds(TOP, rows), pl.ds(0, cols)], local_sem.at[f]
         )
         for f, source, target in ((0, vel_x_ref, vel_x), (1, vel_y_ref, vel_y))
     ]
-    loads.append(
-        pltpu.make_async_copy(outgoing_ref.at[own_tiles], incoming.at[own_tiles], local_sem.at[2])
-    )
     for load in loads:
         load.start()
 
@@ -170,17 +171,34 @@
     lax.fori_loop(1, devices, greet, 0)
     pl.semaphore_wait(barrier, devices - 1)
 
+    def distance(step):
+        return jnp.where(lax.rem(ix, 2) == 0, step, devices - step)
+
+    def tiles_of(device):
+        return pl.ds(pl.multiple_of(device * capacity, capacity), capacity)
+
     def tile_copy(step):
-        other = lax.rem(me + step, devices)
+        away = distance(step)
         return remote(
-            outgoing_ref.at[pl.ds(pl.multiple_of(other * capacity, capacity), capacity)],
-            incoming.at[own_tiles],
-            tile_send_sem.at[step],
-            tile_recv_sem.at[step],
-            partner(step),
-        )
-
-    for load in loads[:2]:
+            outgoing.at[tiles_of(lax.rem(me + away, devices))],
+            incoming.at[tiles_of(me)],
+            tile_send_sem.at[away],
+            tile_recv_sem.at[away],
+            partner(away),
+        )
+
+    def send_tiles(step, carry):
+        first = lax.rem(me + distance(step), devices) * capacity
+        for i in range(capacity):
+            outgoing[first + i] = owned_ref[holder_ref[first + i]]
+        tile_copy(step).start()
+        return carry
+
+    lax.fori_loop(1, devices, send_tiles, 0)
+    for i in range(capacity):
+        incoming[me * capacity + i] = owned_ref[holder_ref[me * capacity + i]]
+
+    for load in loads:
         load.wait()
     face_copies = [
         remote(
@@ -198,12 +216,6 @@
     ]
     for copy in face_copies:
         copy.start()
-
-    def send_tiles(step, carry):
-        tile_copy(step).start()
-        return carry
-
-    lax.fori_loop(1, devices, send_tiles, 0)
 
     for copy in face_copies:
         copy.wait()
@@ -223,6 +235,135 @@
             )
     for copy in side_copies:
         copy.start()
+    row_id = lax.broadcasted_iota(jnp.int32, (tile_rows, tile_cols), 0)
+    col_id = lax.broadcasted_iota(jnp.int32, (tile_rows, tile_cols), 1)
+    weight = jnp.zeros((tile_rows, tile_cols), jnp.float32)
+    for g in range(coefficients_ref.shape[0]):
+        share = coefficients_ref[g]
+        for i in range(faulty_ref.shape[0]):
+            share = jnp.where(faulty_ref[i] == g, 0, share)
+        on_row = (row_id & (jnp.left_shift(1, levels_ref[g, 0]) - 1)) == 0
+        on_col = (col_id & (jnp.left_shift(1, levels_ref[g, 1]) - 1)) == 0
+        weight += jnp.where(on_row & on_col, share.astype(jnp.float32), 0.0)
+
+    def receive_tiles(step, carry):
+        tile_copy(step).wait()
+        return carry
+
+    lax.fori_loop(1, devices, receive_tiles, 0)
+
+    def put(kx, carry):
+        start = pl.multiple_of(TOP + kx * tile_rows, tile_rows)
+        for ky in range(across):
+            slot = kx * across + ky
+            source = me + owner_ref[slot]
+            source = jnp.where(source >= devices, source - devices, source)
+            block[pl.ds(start, tile_rows), ky * tile_cols : (ky + 1) * tile_cols] = (
+                incoming[source * capacity + rank_ref[slot]] * weight
+            )
+        return carry
+
+    lax.fori_loop(0, rows // tile_rows, put, 0, unroll=2)
+
+    def row(point):
+        return block[TOP + point : TOP + point + 1, :]
+
+    def pack_rows(start, nodes):
+        return jnp.concatenate(
+            [row(start + node) for node in nodes]
+            + [jnp.zeros((PACK - len(nodes), cols), jnp.float32)],
+            axis=0,
+        )
+
+    rows_all[ix] = jnp.concatenate(
+        [row(c * CHUNK) for c in range(chunks_x)]
+        + [jnp.zeros((8 - chunks_x, cols), jnp.float32)],
+        axis=0,
+    )
+    row_send[0] = pack_rows(0, FIRST)
+    row_send[1] = pack_rows(rows - CHUNK, LAST)
+    row_copies = [
+        remote(
+            rows_all.at[ix],
+            rows_all.at[ix],
+            rows_sem.at[step, 0],
+            rows_sem.at[step, 1],
+            (lax.rem(ix + step, size_x), iy),
+        )
+        for step in range(1, size_x)
+    ] + [
+        remote(
+            row_send.at[side],
+            row_recv.at[side],
+            row_pack_sem.at[side, 0],
+            row_pack_sem.at[side, 1],
+            device,
+        )
+        for side, device in ((0, before_x), (1, after_x))
+    ]
+    for copy in row_copies:
+        copy.start()
+
+    for c in range(chunks_x):
+        span = slice(TOP + c * CHUNK, TOP + (c + 1) * CHUNK)
+        block[span, :] = split_dot(hats_ref[...], block[span, :], True)
+
+    for copy in row_copies:
+        copy.wait()
+    known = jnp.concatenate(
+        [rows_all[...].reshape(size_x * 8, cols), row_recv[...].reshape(2 * PACK, cols)], axis=0
+    )
+    ends = exact_dot(table_x_ref[ix], known)
+    part = lax.broadcasted_iota(jnp.int32, (CHUNK, 1), 0).astype(jnp.float32) * (1.0 / CHUNK)
+    for c in range(chunks_x):
+        span = slice(TOP + c * CHUNK, TOP + (c + 1) * CHUNK)
+        block[span, :] += (1.0 - part) * ends[c : c + 1] + part * ends[c + 1 : c + 2]
+    block[TOP + rows : TOP + rows + HALO, :] = ends[8:16]
+    block[TOP - HALO : TOP, :] = ends[16:24]
+
+    lane = lax.broadcasted_iota(jnp.int32, (frame, 128), 1)
+    picked = block[:, 0:128]
+    for spot, point in enumerate([128] + [c * CHUNK for c in range(1, chunks_y)]):
+        picked = jnp.where(lane == 10 + spot, block[:, point : point + 1], picked)
+    first = picked.T
+    last_cols = block[:, cols - 128 : cols].T
+    blank = jnp.zeros((8, frame), jnp.float32)
+    cols_all[iy] = jnp.concatenate(
+        [first[0:1], first[11 : 10 + chunks_y], blank[: 8 - chunks_y]], axis=0
+    )
+    col_send[0] = jnp.concatenate(
+        [first[1:9], first[16:17], first[32:33], first[64:65], first[10:11], blank[:4]], axis=0
+    )
+    col_send[1] = jnp.concatenate(
+        [last_cols[node - 128 : node - 127] for node in LAST] + [blank[:4]], axis=0
+    )
+    col_copies = [
+        remote(
+            cols_all.at[iy],
+            cols_all.at[iy],
+            cols_sem.at[step, 0],
+            cols_sem.at[step, 1],
+            (ix, lax.rem(iy + step, size_y)),
+        )
+        for step in range(1, size_y)
+    ] + [
+        remote(
+            col_send.at[side],
+            col_recv.at[side],
+            col_pack_sem.at[side, 0],
+            col_pack_sem.at[side, 1],
+            device,
+        )
+        for side, device in ((0, before_y), (1, after_y))
+    ]
+    for copy in col_copies:
+        copy.start()
+
+    used = rows + 2 * TOP
+    for c in range(chunks_y):
+        span = slice(c * CHUNK, (c + 1) * CHUNK)
+        block[0:used, span] = split_dot(hats_t_ref[...], block[0:used, span], False)
+
     for copy in side_copies:
         copy.wait()
     for f, vel in enumerate((vel_x, vel_y)):
@@ -235,125 +376,6 @@
             axis=0,
         )
         vel[:, cols : cols + 128] = strip.T
-
-    loads[2].wait()
-
-    def receive_tiles(step, carry):
-        tile_copy(step).wait()
-        return carry
-
-    lax.fori_loop(1, devices, receive_tiles, 0)
-
-    weight = weight_ref[...]
-
-    def put(kx, carry):
-        start = pl.multiple_of(TOP + kx * tile_rows, tile_rows)
-        for ky in range(across):
-            block[pl.ds(start, tile_rows), ky * tile_cols : (ky + 1) * tile_cols] = (
-                incoming[place_ref[kx * across + ky]] * weight
-            )
-        return carry
-
-    lax.fori_loop(0, rows // tile_rows, put, 0, unroll=2)
-
-    def row(point):
-        return block[TOP + point : TOP + point + 1, :]
-
-    def pack_rows(start, nodes):
-        return jnp.concatenate(
-            [row(start + node) for node in nodes]
-            + [jnp.zeros((PACK - len(nodes), cols), jnp.float32)],
-            axis=0,
-        )
-
-    rows_all[ix] = jnp.concatenate(
-        [row(c * CHUNK) for c in range(chunks_x)]
-        + [jnp.zeros((8 - chunks_x, cols), jnp.float32)],
-        axis=0,
-    )
-    row_send[0] = pack_rows(0, FIRST)
-    row_send[1] = pack_rows(rows - CHUNK, LAST)
-    row_copies = [
-        remote(
-            rows_all.at[ix],
-            rows_all.at[ix],
-            rows_sem.at[step, 0],
-            rows_sem.at[step, 1],
-            (lax.rem(ix + step, size_x), iy),
-        )
-        for step in range(1, size_x)
-    ] + [
-        remote(
-            row_send.at[side],
-            row_recv.at[side],
-            row_pack_sem.at[side, 0],
-            row_pack_sem.at[side, 1],
-            device,
-        )
-        for side, device in ((0, before_x), (1, after_x))
-    ]
-    for copy in row_copies:
-        copy.start()
-
-    for c in range(chunks_x):
-        span = slice(TOP + c * CHUNK, TOP + (c + 1) * CHUNK)
-        block[span, :] = split_dot(hats_ref[...], block[span, :], True)
-
-    for copy in row_copies:
-        copy.wait()
-    known = jnp.concatenate(
-        [rows_all[...].reshape(size_x * 8, cols), row_recv[...].reshape(2 * PACK, cols)], axis=0
-    )
-    ends = exact_dot(table_x_ref[ix], known)
-    part = lax.broadcasted_iota(jnp.int32, (CHUNK, 1), 0).astype(jnp.float32) * (1.0 / CHUNK)
-    for c in range(chunks_x):
-        span = slice(TOP + c * CHUNK, TOP + (c + 1) * CHUNK)
-        block[span, :] += (1.0 - part) * ends[c : c + 1] + part * ends[c + 1 : c + 2]
-    block[TOP + rows : TOP + rows + HALO, :] = ends[8:16]
-    block[TOP - HALO : TOP, :] = ends[16:24]
-
-    lane = lax.broadcasted_iota(jnp.int32, (frame, 128), 1)
-    picked = block[:, 0:128]
-    for spot, point in enumerate([128] + [c * CHUNK for c in range(1, chunks_y)]):
-        picked = jnp.where(lane == 10 + spot, block[:, point : point + 1], picked)
-    first = picked.T
-    last_cols = block[:, cols - 128 : cols].T
-    blank = jnp.zeros((8, frame), jnp.float32)
-    cols_all[iy] = jnp.concatenate(
-        [first[0:1], first[11 : 10 + chunks_y], blank[: 8 - chunks_y]], axis=0
-    )
-    col_send[0] = jnp.concatenate(
-        [first[1:9], first[16:17], first[32:33], first[64:65], first[10:11], blank[:4]], axis=0
-    )
-    col_send[1] = jnp.concatenate(
-        [last_cols[node - 128 : node - 127] for node in LAST] + [blank[:4]], axis=0
-    )
-    col_copies = [
-        remote(
-            cols_all.at[iy],
-            cols_all.at[iy],
-            cols_sem.at[step, 0],
-            cols_sem.at[step, 1],
-            (ix, lax.rem(iy + step, size_y)),
-        )
-        for step in range(1, size_y)
-    ] + [
-        remote(
-            col_send.at[side],
-            col_recv.at[side],
-            col_pack_sem.at[side, 0],
-            col_pack_sem.at[side, 1],
-            device,
-        )
-        for side, device in ((0, before_y), (1, after_y))
-    ]
-    for copy in col_copies:
-        copy.start()
-
-    used = rows + 2 * TOP
-    for c in range(chunks_y):
-        span = slice(c * CHUNK, (c + 1) * CHUNK)
-        block[0:used, span] = split_dot(hats_t_ref[...], block[0:used, span], False)
 
     for copy in col_copies:
         copy.wait()
@@ -428,15 +450,14 @@
         now, then = then, now
 
 
-def restart(place, weight, outgoing, vel_x, vel_y, size_x, size_y):
+def restart(scalars, owned, vel_x, vel_y, capacity, size_x, size_y):
     rows, cols = vel_x.shape
     frame = (rows + 2 * TOP + 127) // 128 * 128
     devices = size_x * size_y
     hats = hat_matrix()
     operands = (
-        place,
-        weight,
-        outgoing,
+        *scalars,
+        owned,
         vel_x,
         vel_y,
         jnp.asarray(hats.astype(ml_dtypes.bfloat16)),
@@ -445,16 +466,19 @@
         jnp.asarray(frame_table(size_y, cols // CHUNK, 128, 8, 0, 120)),
     )
     vmem = pl.BlockSpec(memory_space=pltpu.VMEM)
+    smem = pl.BlockSpec(memory_space=pltpu.SMEM)
+    tiles = pltpu.VMEM((devices * capacity, *owned.shape[1:]), jnp.float32)
     hbm = pl.BlockSpec(memory_space=pl.ANY)
     dma = pltpu.SemaphoreType.DMA
     framed = pltpu.VMEM((frame, cols + 128), jnp.float32)
     return pl.pallas_call(
         functools.partial(kernel, size_x, size_y),
         out_shape=jax.ShapeDtypeStruct((rows, cols), jnp.float32),
-        in_specs=[pl.BlockSpec(memory_space=pltpu.SMEM), vmem, hbm, hbm, hbm] + [vmem] * 4,
+        in_specs=[smem] * len(scalars) + [vmem, hbm, hbm] + [vmem] * 4,
         out_specs=vmem,
         scratch_shapes=[
-            pltpu.VMEM(outgoing.shape, jnp.float32),
+            tiles,
+            tiles,
             pltpu.VMEM((frame, cols), jnp.float32),
             framed,
             framed,
@@ -486,24 +510,10 @@
     )(*operands)
 
 
-def tile_weights(grid_levels, coefficients, faulty_grids, shape):
-    grid_ids = jnp.arange(coefficients.shape[0], dtype=jnp.int32)
-    alive = jnp.all(faulty_grids[None, :] != grid_ids[:, None], axis=1)
-    share = jnp.where(alive, coefficients, 0).astype(jnp.float32)
-    masks = jnp.left_shift(1, grid_levels) - 1
-    row = jnp.arange(shape[0], dtype=jnp.int32)
-    col = jnp.arange(shape[1], dtype=jnp.int32)
-    on_row = (row[None, :] & masks[:, 0:1]) == 0
-    on_col = (col[None, :] & masks[:, 1:2]) == 0
-    return jnp.sum(
-        jnp.where(on_row[:, :, None] & on_col[:, None, :], share[:, None, None], 0.0), axis=0
-    )
-
-
 def local(
     owned_surplus, tile_owner, grid_levels, coefficients, faulty_grids, velocity_x, velocity_y
 ):
-    slot_count, tile_height, tile_width = owned_surplus.shape
+    slot_count = owned_surplus.shape[0]
     size_x = lax.axis_size("gx")
     size_y = lax.axis_size("gy")
     device_count = size_x * size_y
@@ -518,10 +528,8 @@
     seat = target * capacity + slot_rank
     seats = jnp.arange(device_count * capacity, dtype=jnp.int32)
     holder = jnp.max(jnp.where(seat[None, :] == seats[:, None], positions[None, :], 0), axis=1)
-    outgoing = jnp.take(owned_surplus, holder, axis=0, mode="clip")
-    place = (own_index + offsets) % device_count * capacity + slot_rank
-    weight = tile_weights(grid_levels, coefficients, faulty_grids, (tile_height, tile_width))
-    return restart(place, weight, outgoing, velocity_x, velocity_y, size_x, size_y)
+    scalars = (tile_owner, slot_rank, holder, grid_levels, coefficients, faulty_grids)
+    return restart(scalars, owned_surplus, velocity_x, velocity_y, capacity, size_x, size_y)
 
 
 def solution(mesh):

time: 148 us -> 148 us (level)
  local copies, waits for them, and re-layouts: 5.02 us -> 8.44 us
  other arithmetic: 3.47 us -> 0.99 us
    unnamed x11 -> x16, local copies, waits for them, and re-layouts: 1.35 us -> 7.75 us
    gather x1 -> x0, local copies, waits for them, and re-layouts: 2.97 us -> none  [local(): outgoing = jnp.take(owned_surplus, holder, axis=0, mode='clip')]
where the time goes in v3:
time: 148 us
  Pallas kernels  138 us (93%)
  local copies, waits for them, and re-layouts  8.44 us (6%)
    pallas_call x1, Pallas kernels, restart(): pl.pallas_call(functools.partial(kernel, size_x, size_y), out_shape=jax.S...  138 us
    unnamed x16, local copies, waits for them, and re-layouts  7.75 us

profile of v3, /device:TPU:0, one launch (start us, length us, event | category | flops | bytes accessed | tf_op | source)
XLA Modules:
  0.0 147.7 jit_solution(17862183689602958176)
XLA Ops:
  0.0 0.7 slice.3
  0.7 0.2 convert_reduce_fusion.rank_ref
  0.9 0.7 fusion.2
  1.6 0.1 select_reduce_fusion.holder_ref
  1.7 0.8 copy.13.levels_ref
  2.4 0.0 copy-start
  2.4 1.0 copy-done
  3.5 0.0 copy-start.1
  3.5 0.9 copy-done.1
  4.4 0.0 copy-start.2
  4.4 0.9 copy-done.2
  5.3 0.0 copy-start.3
  5.3 0.8 copy-done.3
  6.1 0.0 copy-start.4
  6.1 0.7 copy-done.4
  6.8 0.0 copy-start.5
  6.8 0.7 copy-done.5
  7.5 0.0 copy-start.6
  7.5 0.7 copy-done.6
  8.1 138.3 %restart.1 = f32[512,1024]{1,0:T(8,128)S(1)} custom-call(s32[4096]{0:T(1024)S(1)} %copy-done.4, s32[128]{0:T(128)S(1)} %convert_reduce_fusion.rank_ref, s32[256]{0:T(256)S(1)} %select_reduce_fusion.holder_ref, s32[8,2]{1,0:T(8,128)S(1)} %copy.13.levels_ref, s32[8]{0:T(128)S(1)} %copy-done.5, s32[2]{0:T(128)S(1)} %copy-done.6, f32[128,16,256]{2,1,0:T(8,128)} %owned_ref.1, ...), custom_call_target="tpu_custom_call" | custom-call | tf_op jit(solution)/shard_map/restart/pallas_call | solution.py:474
  146.4 1.3 copy.15
Async XLA Ops:
  2.4 1.0 copy-start
  3.5 0.9 copy-start.1
  4.4 0.9 copy-start.2
  5.3 0.8 copy-start.3
  6.1 0.7 copy-start.4
  6.8 0.7 copy-start.5
  7.5 0.7 copy-start.6

commit v4 on v3

--- a/solution.py
+++ b/solution.py
@@ -83,20 +83,22 @@
 def kernel(
     size_x,
     size_y,
-    owner_ref,
-    rank_ref,
-    holder_ref,
-    levels_ref,
-    coefficients_ref,
-    faulty_ref,
-    owned_ref,
+    grids,
+    faults,
+    scalars_ref,
+    owned_hbm,
     vel_x_ref,
     vel_y_ref,
+    hats_hbm,
+    hats_t_hbm,
+    table_x_hbm,
+    table_y_hbm,
+    out_ref,
+    owned_ref,
     hats_ref,
     hats_t_ref,
     table_x_ref,
     table_y_ref,
-    out_ref,
     outgoing,
     incoming,
     block,
@@ -127,7 +129,20 @@
     _, tile_rows, tile_cols = owned_ref.shape
     across = cols // tile_cols
     devices = size_x * size_y
+    slots = owned_ref.shape[0]
     capacity = incoming.shape[0] // devices
+    seats = devices * capacity
+    owner_ref, rank_ref, holder_ref, levels_ref, coefficients_ref, faulty_ref = (
+        functools.partial(lambda first, i: scalars_ref[first + i], first)
+        for first in (
+            0,
+            slots,
+            2 * slots,
+            2 * slots + seats,
+            2 * slots + seats + 2 * grids,
+            2 * slots + seats + 3 * grids,
+        )
+    )
     frame = block.shape[0]
     chunks_x = rows // CHUNK
     chunks_y = cols // CHUNK
@@ -159,7 +174,19 @@
         )
         for f, source, target in ((0, vel_x_ref, vel_x), (1, vel_y_ref, vel_y))
     ]
-    for load in loads:
+    tile_load = pltpu.make_async_copy(owned_hbm, owned_ref, local_sem.at[2])
+    table_loads = [
+        pltpu.make_async_copy(source, target, local_sem.at[3 + f])
+        for f, (source, target) in enumerate(
+            (
+                (hats_hbm, hats_ref),
+                (hats_t_hbm, hats_t_ref),
+                (table_x_hbm, table_x_ref),
+                (table_y_hbm, table_y_ref),
+            )
+        )
+    ]
+    for load in [tile_load] + loads + table_loads:
         load.start()
 
     barrier = pltpu.get_barrier_semaphore()
@@ -190,13 +217,14 @@
     def send_tiles(step, carry):
         first = lax.rem(me + distance(step), devices) * capacity
         for i in range(capacity):
-            outgoing[first + i] = owned_ref[holder_ref[first + i]]
+            outgoing[first + i] = owned_ref[holder_ref(first + i)]
         tile_copy(step).start()
         return carry
 
+    tile_load.wait()
     lax.fori_loop(1, devices, send_tiles, 0)
     for i in range(capacity):
-        incoming[me * capacity + i] = owned_ref[holder_ref[me * capacity + i]]
+        incoming[me * capacity + i] = owned_ref[holder_ref(me * capacity + i)]
 
     for load in loads:
         load.wait()
@@ -219,6 +247,15 @@
 
     for copy in face_copies:
         copy.wait()
+    scale = TIME_STEP / 12.0
+
+    def scale_rows(i, carry):
+        span = pl.ds(pl.multiple_of(TOP - HALO + i * 16, 8), 16)
+        for vel in (vel_x, vel_y):
+            vel[span, 0:cols] = vel[span, 0:cols] * (8.0 * scale)
+        return carry
+
+    lax.fori_loop(0, (rows + 2 * HALO) // 16, scale_rows, 0)
     side_copies = []
     for f, vel in enumerate((vel_x, vel_y)):
         side_send[f, 0] = vel[:, 0:128].T[0:HALO]
@@ -238,13 +275,16 @@
     row_id = lax.broadcasted_iota(jnp.int32, (tile_rows, tile_cols), 0)
     col_id = lax.broadcasted_iota(jnp.int32, (tile_rows, tile_cols), 1)
     weight = jnp.zeros((tile_rows, tile_cols), jnp.float32)
-    for g in range(coefficients_ref.shape[0]):
-        share = coefficients_ref[g]
-        for i in range(faulty_ref.shape[0]):
-            share = jnp.where(faulty_ref[i] == g, 0, share)
-        on_row = (row_id & (jnp.left_shift(1, levels_ref[g, 0]) - 1)) == 0
-        on_col = (col_id & (jnp.left_shift(1, levels_ref[g, 1]) - 1)) == 0
+    for g in range(grids):
+        share = coefficients_ref(g)
+        for i in range(faults):
+            share = jnp.where(faulty_ref(i) == g, 0, share)
+        on_row = (row_id & (jnp.left_shift(1, levels_ref(2 * g)) - 1)) == 0
+        on_col = (col_id & (jnp.left_shift(1, levels_ref(2 * g + 1)) - 1)) == 0
         weight += jnp.where(on_row & on_col, share.astype(jnp.float32), 0.0)
+
+    for load in table_loads:
+        load.wait()
 
     def receive_tiles(step, carry):
         tile_copy(step).wait()
@@ -256,10 +296,10 @@
         start = pl.multiple_of(TOP + kx * tile_rows, tile_rows)
         for ky in range(across):
             slot = kx * across + ky
-            source = me + owner_ref[slot]
+            source = me + owner_ref(slot)
             source = jnp.where(source >= devices, source - devices, source)
             block[pl.ds(start, tile_rows), ky * tile_cols : (ky + 1) * tile_cols] = (
-                incoming[source * capacity + rank_ref[slot]] * weight
+                incoming[source * capacity + rank_ref(slot)] * weight
             )
         return carry
 
@@ -394,13 +434,13 @@
         )
 
     width = cols + 128
-    scale = TIME_STEP / 12.0
-
-    def change(ref, start):
-        around = ref.at[pl.ds(pl.multiple_of(start - 8, 8), 24), :]
+    group = 16
+
+    def advance(ref, start):
+        around = ref.at[pl.ds(pl.multiple_of(start - 8, 8), group + 16), :]
 
         def read(shift):
-            return around[8 + shift : 16 + shift, :]
+            return around[8 + shift : 8 + group + shift, :]
 
         centre = read(0)
         west_one, east_one = read(-1), read(1)
@@ -411,60 +451,56 @@
         south_two = pltpu.roll(centre, 2, 1)
         near = (east_one + west_one) + (north_one + south_one)
         far = (east_two + west_two) + (north_two + south_two)
-        slope_x = 8.0 * (east_one - west_one) - (east_two - west_two)
-        slope_y = 8.0 * (north_one - south_one) - (north_two - south_two)
-        total = (8.0 * near - 0.5 * far - 30.0 * centre) - (
-            vel_x[pl.ds(start, 8), :] * slope_x + vel_y[pl.ds(start, 8), :] * slope_y
-        )
-        return centre, scale * total
+        slope_x = (east_one - west_one) - 0.125 * (east_two - west_two)
+        slope_y = (north_one - south_one) - 0.125 * (north_two - south_two)
+        span = pl.ds(start, group)
+        moved = vel_x[span, :] * slope_x + vel_y[span, :] * slope_y
+        return (
+            (1.0 - 30.0 * scale) * centre + ((8.0 * scale) * near - (0.5 * scale) * far) - moved
+        )
 
     def sweep(start, count, body):
         def strip(i, carry):
-            body(pl.multiple_of(start + i * 8, 8))
+            body(pl.multiple_of(start + i * group, 8))
             return carry
 
-        group = next(g for g in (8, 6, 4, 3, 2, 1) if count % g == 0)
-        lax.fori_loop(0, count, strip, 0, unroll=group)
+        unroll = next(g for g in (4, 3, 2, 1) if count % g == 0)
+        lax.fori_loop(0, count, strip, 0, unroll=unroll)
 
     now, then = field, later
     for step in range(STEPS):
         last = step == STEPS - 1
 
         def first_half(start, now=now):
-            centre, delta = change(now, start)
-            middle[pl.ds(start, 8), :] = centre + delta
+            middle[pl.ds(start, group), :] = advance(now, start)
 
         def second_half(start, now=now, then=then, last=last):
-            centre, delta = change(middle, start)
-            value = 0.5 * (now[pl.ds(start, 8), :] + centre + delta)
+            value = 0.5 * (now[pl.ds(start, group), :] + advance(middle, start))
             if last:
-                out_ref[pl.ds(pl.multiple_of(start - TOP, 8), 8), :] = value[:, :cols]
+                out_ref[pl.ds(pl.multiple_of(start - TOP, 8), group), :] = value[:, :cols]
             else:
-                then[pl.ds(start, 8), :] = value
-
-        sweep(TOP - HALO, (rows + 2 * HALO) // 8, first_half)
+                then[pl.ds(start, group), :] = value
+
+        sweep(TOP - HALO, (rows + 2 * HALO) // group, first_half)
         if last:
-            sweep(TOP, rows // 8, second_half)
+            sweep(TOP, rows // group, second_half)
         else:
-            sweep(TOP - HALO, (rows + 2 * HALO) // 8, second_half)
+            sweep(TOP - HALO, (rows + 2 * HALO) // group, second_half)
         now, then = then, now
 
 
-def restart(scalars, owned, vel_x, vel_y, capacity, size_x, size_y):
+def restart(scalars, owned, vel_x, vel_y, capacity, grids, faults, size_x, size_y):
     rows, cols = vel_x.shape
     frame = (rows + 2 * TOP + 127) // 128 * 128
     devices = size_x * size_y
     hats = hat_matrix()
-    operands = (
-        *scalars,
-        owned,
-        vel_x,
-        vel_y,
+    tables = (
         jnp.asarray(hats.astype(ml_dtypes.bfloat16)),
         jnp.asarray(hats.T.astype(ml_dtypes.bfloat16)),
         jnp.asarray(frame_table(size_x, rows // CHUNK, 24, 0, 8, 16)),
         jnp.asarray(frame_table(size_y, cols // CHUNK, 128, 8, 0, 120)),
     )
+    operands = (scalars, owned, vel_x, vel_y, *tables)
     vmem = pl.BlockSpec(memory_space=pltpu.VMEM)
     smem = pl.BlockSpec(memory_space=pltpu.SMEM)
     tiles = pltpu.VMEM((devices * capacity, *owned.shape[1:]), jnp.float32)
@@ -472,11 +508,13 @@
     dma = pltpu.SemaphoreType.DMA
     framed = pltpu.VMEM((frame, cols + 128), jnp.float32)
     return pl.pallas_call(
-        functools.partial(kernel, size_x, size_y),
+        functools.partial(kernel, size_x, size_y, grids, faults),
         out_shape=jax.ShapeDtypeStruct((rows, cols), jnp.float32),
-        in_specs=[smem] * len(scalars) + [vmem, hbm, hbm] + [vmem] * 4,
+        in_specs=[smem] + [hbm] * 7,
         out_specs=vmem,
         scratch_shapes=[
+            pltpu.VMEM(owned.shape, jnp.float32),
+            *(pltpu.VMEM(table.shape, table.dtype) for table in tables),
             tiles,
             tiles,
             pltpu.VMEM((frame, cols), jnp.float32),
@@ -493,7 +531,7 @@
             pltpu.VMEM((2, PACK, frame), jnp.float32),
             pltpu.VMEM((2, 2, HALO, frame), jnp.float32),
             pltpu.VMEM((2, 2, HALO, frame), jnp.float32),
-            dma((3,)),
+            dma((7,)),
             dma((devices,)),
             dma((devices,)),
             dma((size_x, 2)),
@@ -528,8 +566,20 @@
     seat = target * capacity + slot_rank
     seats = jnp.arange(device_count * capacity, dtype=jnp.int32)
     holder = jnp.max(jnp.where(seat[None, :] == seats[:, None], positions[None, :], 0), axis=1)
-    scalars = (tile_owner, slot_rank, holder, grid_levels, coefficients, faulty_grids)
-    return restart(scalars, owned_surplus, velocity_x, velocity_y, capacity, size_x, size_y)
+    scalars = jnp.concatenate(
+        [offsets, slot_rank, holder, grid_levels.reshape(-1), coefficients, faulty_grids]
+    )
+    return restart(
+        scalars,
+        owned_surplus,
+        velocity_x,
+        velocity_y,
+        capacity,
+        coefficients.shape[0],
+        faulty_grids.shape[0],
+        size_x,
+        size_y,
+    )
 
 
 def solution(mesh):

time: 148 us -> 143 us (0.966)
  Pallas kernels: 138 us -> 135 us
    pallas_call x1, Pallas kernels: 138 us -> 135 us  [restart(): pl.pallas_call(functools.partial(kernel, size_x, size_y, grids, faults),...]
    unnamed x16 -> x10, local copies, waits for them, and re-layouts: 7.75 us -> 5.72 us
where the time goes in v4:
time: 143 us
  Pallas kernels  135 us (94%)
  local copies, waits for them, and re-layouts  7.24 us (5%)
    pallas_call x1, Pallas kernels, restart(): pl.pallas_call(functools.partial(kernel, size_x, size_y, grids, faults),...  135 us
    unnamed x10, local copies, waits for them, and re-layouts  5.72 us

profile of v4, /device:TPU:0, one launch (start us, length us, event | category | flops | bytes accessed | tf_op | source)
XLA Modules:
  0.0 142.9 jit_solution(14303426709712775530)
XLA Ops:
  0.0 0.7 slice.3
  0.7 0.2 convert_reduce_fusion
  0.9 0.7 fusion.2
  1.6 0.1 select_reduce_fusion
  1.7 0.8 copy.14
  2.4 0.1 reshape.6
  2.5 0.7 concatenate.3.scalars_ref
  3.3 0.0 copy-start
  3.3 1.0 copy-done
  4.3 0.0 copy-start.1
  4.3 0.9 copy-done.1
  5.2 0.0 copy-start.2
  5.2 0.9 copy-done.2
  6.1 0.0 copy-start.3
  6.1 0.8 copy-done.3
  6.9 134.7 %restart.1 = f32[512,1024]{1,0:T(8,128)S(1)} custom-call(s32[538]{0:T(1024)S(1)} %concatenate.3.scalars_ref, f32[128,16,256]{2,1,0:T(8,128)} %owned_hbm.1, f32[512,1024]{1,0:T(8,128)} %vel_x_ref.1, f32[512,1024]{1,0:T(8,128)} %vel_y_ref.1, bf16[256,256]{1,0:T(8,128)(2,1)S(1)} %copy-done.2, bf16[256,256]{1,0:T(8,128)(2,1)S(1)} %copy-done.1, ...), custom_call_target="tpu_custom_call" | custom-call | tf_op jit(solution)/shard_map/restart/pallas_call | solution.py:510
  141.6 1.3 copy.16
Async XLA Ops:
  3.3 1.0 copy-start
  4.3 0.9 copy-start.1
  5.2 0.9 copy-start.2
  6.1 0.8 copy-start.3

commit v5 on v4

--- a/solution.py
+++ b/solution.py
@@ -2,7 +2,6 @@
 
 import jax
 import jax.numpy as jnp
-import ml_dtypes
 import numpy as np
 from jax import lax
 from jax.experimental import pallas as pl
@@ -64,6 +63,18 @@
     return table.astype(np.float32)
 
 
+def hats_of(points_dim):
+    points = lax.broadcasted_iota(jnp.int32, (CHUNK, CHUNK), points_dim)
+    nodes = lax.broadcasted_iota(jnp.int32, (CHUNK, CHUNK), 1 - points_dim)
+    slope = jnp.ones((CHUNK, CHUNK), jnp.float32)
+    reach = 2
+    while reach < CHUNK:
+        slope = jnp.where((nodes & (reach - 1)) == 0, 1.0 / reach, slope)
+        reach *= 2
+    hats = jnp.maximum(1.0 - jnp.abs(points - nodes).astype(jnp.float32) * slope, 0.0)
+    return jnp.where(nodes == 0, 0.0, hats).astype(jnp.bfloat16)
+
+
 def split_dot(matrix, values, left):
     high = values.astype(jnp.bfloat16)
     low = (values - high.astype(jnp.float32)).astype(jnp.bfloat16)
@@ -89,16 +100,12 @@
     owned_hbm,
     vel_x_ref,
     vel_y_ref,
-    hats_hbm,
-    hats_t_hbm,
-    table_x_hbm,
-    table_y_hbm,
+    tables_hbm,
     out_ref,
     owned_ref,
     hats_ref,
     hats_t_ref,
-    table_x_ref,
-    table_y_ref,
+    tables_ref,
     outgoing,
     incoming,
     block,
@@ -175,17 +182,7 @@
         for f, source, target in ((0, vel_x_ref, vel_x), (1, vel_y_ref, vel_y))
     ]
     tile_load = pltpu.make_async_copy(owned_hbm, owned_ref, local_sem.at[2])
-    table_loads = [
-        pltpu.make_async_copy(source, target, local_sem.at[3 + f])
-        for f, (source, target) in enumerate(
-            (
-                (hats_hbm, hats_ref),
-                (hats_t_hbm, hats_t_ref),
-                (table_x_hbm, table_x_ref),
-                (table_y_hbm, table_y_ref),
-            )
-        )
-    ]
+    table_loads = [pltpu.make_async_copy(tables_hbm, tables_ref, local_sem.at[3])]
     for load in [tile_load] + loads + table_loads:
         load.start()
 
@@ -279,12 +276,14 @@
         share = coefficients_ref(g)
         for i in range(faults):
             share = jnp.where(faulty_ref(i) == g, 0, share)
-        on_row = (row_id & (jnp.left_shift(1, levels_ref(2 * g)) - 1)) == 0
-        on_col = (col_id & (jnp.left_shift(1, levels_ref(2 * g + 1)) - 1)) == 0
+        on_row = (row_id & (jnp.left_shift(1, levels_ref(g)) - 1)) == 0
+        on_col = (col_id & (jnp.left_shift(1, levels_ref(grids + g)) - 1)) == 0
         weight += jnp.where(on_row & on_col, share.astype(jnp.float32), 0.0)
 
     for load in table_loads:
         load.wait()
+    hats_ref[...] = hats_of(0)
+    hats_t_ref[...] = hats_of(1)
 
     def receive_tiles(step, carry):
         tile_copy(step).wait()
@@ -353,7 +352,7 @@
     known = jnp.concatenate(
         [rows_all[...].reshape(size_x * 8, cols), row_recv[...].reshape(2 * PACK, cols)], axis=0
     )
-    ends = exact_dot(table_x_ref[ix], known)
+    ends = exact_dot(tables_ref[pl.ds(size_y * 128 + ix * 24, 24), 0 : size_x * 8 + 2 * PACK], known)
     part = lax.broadcasted_iota(jnp.int32, (CHUNK, 1), 0).astype(jnp.float32) * (1.0 / CHUNK)
     for c in range(chunks_x):
         span = slice(TOP + c * CHUNK, TOP + (c + 1) * CHUNK)
@@ -422,7 +421,7 @@
     known = jnp.concatenate(
         [cols_all[...].reshape(size_y * 8, frame), col_recv[...].reshape(2 * PACK, frame)], axis=0
     )
-    ends = exact_dot(table_y_ref[iy], known).T
+    ends = exact_dot(tables_ref[pl.ds(iy * 128, 128), :], known).T
     field[:, cols : cols + 128] = ends
     part = lax.broadcasted_iota(jnp.int32, (1, CHUNK), 1).astype(jnp.float32) * (1.0 / CHUNK)
     for c in range(chunks_y):
@@ -434,9 +433,8 @@
         )
 
     width = cols + 128
-    group = 16
-
-    def advance(ref, start):
+
+    def advance(ref, start, group):
         around = ref.at[pl.ds(pl.multiple_of(start - 8, 8), group + 16), :]
 
         def read(shift):
@@ -459,33 +457,34 @@
             (1.0 - 30.0 * scale) * centre + ((8.0 * scale) * near - (0.5 * scale) * far) - moved
         )
 
-    def sweep(start, count, body):
+    def sweep(start, length, body):
+        group = next(g for g in (48, 32, 16, 8) if length % g == 0)
+
         def strip(i, carry):
-            body(pl.multiple_of(start + i * group, 8))
+            body(pl.multiple_of(start + i * group, 8), group)
             return carry
 
-        unroll = next(g for g in (4, 3, 2, 1) if count % g == 0)
-        lax.fori_loop(0, count, strip, 0, unroll=unroll)
+        lax.fori_loop(0, length // group, strip, 0)
 
     now, then = field, later
     for step in range(STEPS):
         last = step == STEPS - 1
 
-        def first_half(start, now=now):
-            middle[pl.ds(start, group), :] = advance(now, start)
-
-        def second_half(start, now=now, then=then, last=last):
-            value = 0.5 * (now[pl.ds(start, group), :] + advance(middle, start))
+        def first_half(start, group, now=now):
+            middle[pl.ds(start, group), :] = advance(now, start, group)
+
+        def second_half(start, group, now=now, then=then, last=last):
+            value = 0.5 * (now[pl.ds(start, group), :] + advance(middle, start, group))
             if last:
                 out_ref[pl.ds(pl.multiple_of(start - TOP, 8), group), :] = value[:, :cols]
             else:
                 then[pl.ds(start, group), :] = value
 
-        sweep(TOP - HALO, (rows + 2 * HALO) // group, first_half)
+        sweep(TOP - HALO, rows + 2 * HALO, first_half)
         if last:
-            sweep(TOP, rows // group, second_half)
+            sweep(TOP, rows, second_half)
         else:
-            sweep(TOP - HALO, (rows + 2 * HALO) // group, second_half)
+            sweep(TOP - HALO, rows + 2 * HALO, second_half)
         now, then = then, now
 
 
@@ -493,14 +492,14 @@
     rows, cols = vel_x.shape
     frame = (rows + 2 * TOP + 127) // 128 * 128
     devices = size_x * size_y
-    hats = hat_matrix()
-    tables = (
-        jnp.asarray(hats.astype(ml_dtypes.bfloat16)),
-        jnp.asarray(hats.T.astype(ml_dtypes.bfloat16)),
-        jnp.asarray(frame_table(size_x, rows // CHUNK, 24, 0, 8, 16)),
-        jnp.asarray(frame_table(size_y, cols // CHUNK, 128, 8, 0, 120)),
-    )
-    operands = (scalars, owned, vel_x, vel_y, *tables)
+    table_x = frame_table(size_x, rows // CHUNK, 24, 0, 8, 16)
+    table_y = frame_table(size_y, cols // CHUNK, 128, 8, 0, 120)
+    wider = table_y.shape[2] - table_x.shape[2]
+    table_x = np.pad(table_x, ((0, 0), (0, 0), (0, wider)))
+    tables = jnp.asarray(
+        np.concatenate([table.reshape(-1, table.shape[2]) for table in (table_y, table_x)])
+    )
+    operands = (scalars, owned, vel_x, vel_y, tables)
     vmem = pl.BlockSpec(memory_space=pltpu.VMEM)
     smem = pl.BlockSpec(memory_space=pltpu.SMEM)
     tiles = pltpu.VMEM((devices * capacity, *owned.shape[1:]), jnp.float32)
@@ -510,11 +509,13 @@
     return pl.pallas_call(
         functools.partial(kernel, size_x, size_y, grids, faults),
         out_shape=jax.ShapeDtypeStruct((rows, cols), jnp.float32),
-        in_specs=[smem] + [hbm] * 7,
+        in_specs=[smem] + [hbm] * 4,
         out_specs=vmem,
         scratch_shapes=[
             pltpu.VMEM(owned.shape, jnp.float32),
-            *(pltpu.VMEM(table.shape, table.dtype) for table in tables),
+            pltpu.VMEM((CHUNK, CHUNK), jnp.bfloat16),
+            pltpu.VMEM((CHUNK, CHUNK), jnp.bfloat16),
+            pltpu.VMEM(tables.shape, jnp.float32),
             tiles,
             tiles,
             pltpu.VMEM((frame, cols), jnp.float32),
@@ -531,7 +532,7 @@
             pltpu.VMEM((2, PACK, frame), jnp.float32),
             pltpu.VMEM((2, 2, HALO, frame), jnp.float32),
             pltpu.VMEM((2, 2, HALO, frame), jnp.float32),
-            dma((7,)),
+            dma((4,)),
             dma((devices,)),
             dma((devices,)),
             dma((size_x, 2)),
@@ -567,7 +568,7 @@
     seats = jnp.arange(device_count * capacity, dtype=jnp.int32)
     holder = jnp.max(jnp.where(seat[None, :] == seats[:, None], positions[None, :], 0), axis=1)
     scalars = jnp.concatenate(
-        [offsets, slot_rank, holder, grid_levels.reshape(-1), coefficients, faulty_grids]
+        [offsets, slot_rank, holder, grid_levels.T.reshape(-1), coefficients, faulty_grids]
     )
     return restart(
         scalars,

time: 143 us -> 142 us (level)
  local copies, waits for them, and re-layouts: 7.24 us -> 4.58 us
    unnamed x10 -> x3, local copies, waits for them, and re-layouts: 5.72 us -> 2.38 us
where the time goes in v5:
time: 142 us; the launch traced here: 141 us
  Pallas kernels  136 us (96%)
  local copies, waits for them, and re-layouts  4.58 us (3%)
    pallas_call x1, Pallas kernels, restart(): pl.pallas_call(functools.partial(kernel, size_x, size_y, grids, faults),...  136 us

profile of v5, /device:TPU:0, one launch (start us, length us, event | category | flops | bytes accessed | tf_op | source)
XLA Modules:
  0.0 141.4 jit_solution(2834288845103064924)
XLA Ops:
  0.0 0.7 slice.3
  0.7 0.2 convert_reduce_fusion
  0.9 0.7 fusion.2
  1.6 0.1 select_reduce_fusion
  1.7 0.8 reshape.6
  2.5 0.7 concatenate.3.scalars_ref
  3.2 0.0 copy-start
  3.2 1.1 copy-done
  4.3 135.8 %restart.1 = f32[512,1024]{1,0:T(8,128)S(1)} custom-call(s32[538]{0:T(1024)S(1)} %concatenate.3.scalars_ref, f32[128,16,256]{2,1,0:T(8,128)} %owned_hbm.1, f32[512,1024]{1,0:T(8,128)} %vel_x_ref.1, f32[512,1024]{1,0:T(8,128)} %vel_y_ref.1, f32[1120,96]{1,0:T(8,128)S(1)} %copy-done), custom_call_target="tpu_custom_call" | custom-call | tf_op jit(solution)/shard_map/restart/pallas_call | solution.py:509
  140.0 1.3 copy.10
Async XLA Ops:
  3.2 1.1 copy-start

commit v6 on v5

--- a/solution.py
+++ b/solution.py
@@ -458,13 +458,15 @@
         )
 
     def sweep(start, length, body):
-        group = next(g for g in (48, 32, 16, 8) if length % g == 0)
+        group = 16 if length % 16 == 0 else 8
+        count = length // group
 
         def strip(i, carry):
             body(pl.multiple_of(start + i * group, 8), group)
             return carry
 
-        lax.fori_loop(0, length // group, strip, 0)
+        unroll = next(g for g in (4, 3, 2, 1) if count % g == 0)
+        lax.fori_loop(0, count, strip, 0, unroll=unroll)
 
     now, then = field, later
     for step in range(STEPS):

time: 142 us -> 140 us (0.986)
  Pallas kernels: 136 us -> 134 us
    pallas_call x1, Pallas kernels: 136 us -> 134 us  [restart(): pl.pallas_call(functools.partial(kernel, size_x, size_y, grids, faults),...]
where the time goes in v6:
time: 140 us
  Pallas kernels  134 us (96%)
  local copies, waits for them, and re-layouts  4.58 us (3%)
    pallas_call x1, Pallas kernels, restart(): pl.pallas_call(functools.partial(kernel, size_x, size_y, grids, faults),...  134 us

profile of v6, /device:TPU:0, one launch (start us, length us, event | category | flops | bytes accessed | tf_op | source)
XLA Modules:
  0.0 139.9 jit_solution(11032626271063706761)
XLA Ops:
  0.0 0.7 slice.3
  0.7 0.2 convert_reduce_fusion
  0.9 0.7 fusion.2
  1.6 0.1 select_reduce_fusion
  1.7 0.8 reshape.6
  2.5 0.7 concatenate.3.scalars_ref
  3.2 0.0 copy-start
  3.2 1.1 copy-done
  4.3 134.3 %restart.1 = f32[512,1024]{1,0:T(8,128)S(1)} custom-call(s32[538]{0:T(1024)S(1)} %concatenate.3.scalars_ref, f32[128,16,256]{2,1,0:T(8,128)} %owned_hbm.1, f32[512,1024]{1,0:T(8,128)} %vel_x_ref.1, f32[512,1024]{1,0:T(8,128)} %vel_y_ref.1, f32[1120,96]{1,0:T(8,128)S(1)} %copy-done), custom_call_target="tpu_custom_call" | custom-call | tf_op jit(solution)/shard_map/restart/pallas_call | solution.py:511
  138.6 1.3 copy.10
Async XLA Ops:
  3.2 1.1 copy-start
